TPU v7x, 32 devices: a whole 2x2x4 slice. The times are simulated.
32 devices in a mesh: grp: 4 (over x, core), dev: 8 (over z, y).
Axes of the slice: x: 2, y: 2, z: 4, core: 2. Of those that a mesh axis runs over, the one named last changes fastest.
Arguments:
- amplitudes: bfloat16 [32, 128, 128], P(('grp', 'dev')), may hold values from -2 to 2
- bases: bfloat16 [32, 256, 128], P(('grp', 'dev')), may hold values from -0.375 to 0.375
- factors: bfloat16 [32, 32, 256, 256], P(('grp', 'dev')), may hold values from -0.1875 to 0.1875
- intersections: bfloat16 [32, 4, 128, 128], P(('grp', 'dev')), may hold values from -0.25 to 0.25
- pair_integrals: float32 [32, 128, 128], P(('grp', 'dev')), may hold values from -6 to 6
- pno_energies: float32 [32, 128], P(('grp', 'dev')), may hold values from 0.3 to 3
- pair_shift: float32 [32], P(('grp', 'dev')), may hold values from 0.5 to 4
- pair_atoms: int32 [32, 2], P('grp'), may hold values from 0 to 7, all different within a row; in each aligned block of 8 rows (0 to 7, 8 to 15, ...) at most 3 rows name the same one
- pair_next: int32 [32, 4], P(('grp', 'dev')), may hold values from 0 to 15, as said below
Outputs:
- new_amplitudes: float32 [32, 128, 128], P(('grp', 'dev'))
Inputs may be any that keep to these rules, and one draw needn't show every extreme that they name: `pair_atoms`: each pair lists 2 different atoms of its own group. Within a group no atom is listed by more than 3 pairs, and some atom is listed by exactly 3 pairs of its group. `pair_next`: each pair lists 4 different pairs other than itself; a number below 8 is a pair of its own group, a number m from 8 on is pair m - 8 of the next group. Pairs of the last group list only pairs of their own group.
All inputs are finite; a program needn't handle non-finite values.
Results may differ from a plain program's by a relative error of at most 0.008.
Values may be sent and summed in bfloat16 or wider, within the bound.
No kernel may reach another device: no remote copies, remote signals or barrier semaphores. Data moves between devices by JAX's collectives and lax.ppermute only.
A program may use at most 128 MiB of HBM per device.

v0:
```python
import jax
import jax.numpy as jnp
from jax import lax
from jax.experimental import pallas as pl
from jax.experimental.pallas import tpu as pltpu
from jax.sharding import PartitionSpec as P

CAP = 3
ITERS = 2
F32 = jnp.float32
BF16 = jnp.bfloat16


def vmem_spec():
    return pl.BlockSpec(memory_space=pltpu.VMEM)


def smem_spec():
    return pl.BlockSpec(memory_space=pltpu.SMEM)


def params(mib):
    return pltpu.CompilerParams(vmem_limit_bytes=mib * 2**20)


def exchange(value, axis, offset):
    count = lax.axis_size(axis)
    return lax.ppermute(value, axis, [(d, d ^ offset) for d in range(count)])


def gather_across(value, axis):
    other = exchange(value, axis, lax.axis_size(axis) // 2)
    return jnp.concatenate([value, other], axis=0)


def gather_near(pair, axis):
    half = lax.axis_size(axis) // 2
    return [pair] + [exchange(pair, axis, j) for j in range(1, half)]


def from_next(value, axis):
    count = lax.axis_size(axis)
    return lax.ppermute(value, axis, [(d, d - 1) for d in range(1, count)])


def project_kernel(given, slots, *refs):
    base_refs, (factors_ref, out_ref, wide, narrow, half) = refs[:given], refs[given:]
    aux, npno = factors_ref.shape[0], narrow.shape[2]

    @pl.when(pl.program_id(0) == 0)
    def _():
        for s in range(CAP):
            for j in range(given):

                @pl.when(lax.rem(slots[s], given) == j)
                def _():
                    narrow[s] = base_refs[j][slots[s] // given]

            wide[pl.ds(s * npno, npno), :] = narrow[s].astype(F32).T.astype(BF16)

    for k in range(aux):
        left = jnp.dot(wide[...], factors_ref[k], preferred_element_type=F32).astype(BF16)
        for s in range(CAP):
            half[s, pl.ds(k * npno, npno), :] = left[s * npno : (s + 1) * npno]
    for s in range(CAP):
        both = jnp.dot(half[s], narrow[s], preferred_element_type=F32).astype(BF16)
        for k in range(aux):
            out_ref[s, k // 2, :, pl.ds((k % 2) * npno, npno)] = both[k * npno : (k + 1) * npno]


def project(slots, group_bases, factor_block, step=8):
    aux, width, _ = factor_block.shape
    given = len(group_bases)
    npno = group_bases[0].shape[2]
    step = min(step, aux)

    def kernel(*refs):
        project_kernel(given, *refs)

    return pl.pallas_call(
        kernel,
        grid=(aux // step,),
        in_specs=[smem_spec()]
        + [pl.BlockSpec((2, width, npno), lambda i: (0, 0, 0))] * given
        + [pl.BlockSpec((step, width, width), lambda i: (i, 0, 0))],
        out_specs=pl.BlockSpec((CAP, step // 2, npno, 2 * npno), lambda i: (0, i, 0, 0)),
        out_shape=jax.ShapeDtypeStruct((CAP, aux // 2, npno, 2 * npno), BF16),
        scratch_shapes=[
            pltpu.VMEM((CAP * npno, width), BF16),
            pltpu.VMEM((CAP, width, npno), BF16),
            pltpu.VMEM((CAP, step * npno, width), BF16),
        ],
        compiler_params=params(48),
        cost_estimate=pl.CostEstimate(
            flops=4 * CAP * aux * npno * width * (width + npno) // 2,
            bytes_accessed=2 * aux * width * width,
            transcendentals=0,
        ),
        name="project",
    )(slots, *group_bases, factor_block)


def ladder_kernel(given, slots, pairs, *refs):
    amp_refs, (proj_ref, out_ref, twice, mixed, narrow, sems) = refs[:given], refs[given:]
    half, npno = proj_ref.shape[1], proj_ref.shape[2]
    s = pl.program_id(0)

    @pl.when(s == 0)
    def _():
        twice[...] = jnp.zeros_like(twice)

    for j in range(given):

        @pl.when(lax.rem(slots[s], given) == j)
        def _():
            amp = amp_refs[j][slots[s] // given]
            twice[pl.ds(0, npno), pl.ds(0, npno)] = amp
            twice[pl.ds(npno, npno), pl.ds(npno, npno)] = amp

    flat = proj_ref[0].reshape(half * npno, 2 * npno)
    mixed[...] = jnp.dot(flat, twice[...], preferred_element_type=F32).astype(BF16)
    total = jnp.zeros((npno, npno), F32)
    for m in range(half):
        total = total + lax.dot_general(
            mixed[pl.ds(m * npno, npno), :],
            proj_ref[0, m],
            (((1,), (1,)), ((), ())),
            preferred_element_type=F32,
        )
    narrow[s] = total.astype(BF16)

    def copy(t):
        return pltpu.make_async_copy(narrow.at[t], out_ref.at[jnp.maximum(pairs[t], 0)], sems.at[t])

    @pl.when(pairs[s] >= 0)
    def _():
        copy(s).start()

    @pl.when(s == CAP - 1)
    def _():
        for t in range(CAP):

            @pl.when(pairs[t] >= 0)
            def _():
                copy(t).wait()


def ladder(count, slots, pairs, group_amps, projected):
    given = len(group_amps)
    npno = group_amps[0].shape[1]
    half = projected.shape[1]

    def kernel(*refs):
        ladder_kernel(given, *refs)

    return pl.pallas_call(
        kernel,
        grid=(CAP,),
        in_specs=[smem_spec()] * 2
        + [pl.BlockSpec(group_amps[0].shape, lambda s: (0, 0, 0))] * given
        + [pl.BlockSpec((1, half, npno, 2 * npno), lambda s: (s, 0, 0, 0))],
        out_specs=pl.BlockSpec(memory_space=pl.ANY),
        out_shape=jax.ShapeDtypeStruct((count, npno, npno), BF16),
        scratch_shapes=[
            pltpu.VMEM((2 * npno, 2 * npno), BF16),
            pltpu.VMEM((half * npno, 2 * npno), BF16),
            pltpu.VMEM((CAP, npno, npno), BF16),
            pltpu.SemaphoreType.DMA((CAP,)),
        ],
        compiler_params=params(24),
        cost_estimate=pl.CostEstimate(
            flops=0,
            bytes_accessed=16 * CAP * half * npno**2,
            transcendentals=0,
        ),
        name="ladder",
    )(slots, pairs, *group_amps, projected)


def coupling_kernel(near, own_ref, next_ref, inter_ref, ints_ref, out_ref):
    count = own_ref.shape[0]
    total = ints_ref[...]
    for n in range(inter_ref.shape[0]):
        at = near[n]
        own = own_ref[jnp.minimum(at, count - 1)]
        far = next_ref[jnp.maximum(at - count, 0)]
        amp = jnp.where(at < count, own, far)
        inter = inter_ref[n]
        mixed = jnp.dot(inter, amp, preferred_element_type=F32).astype(BF16)
        total = total + lax.dot_general(
            mixed, inter, (((1,), (1,)), ((), ())), preferred_element_type=F32
        )
    out_ref[...] = total


def coupling(near, own, following, inter, ints):
    return pl.pallas_call(
        coupling_kernel,
        in_specs=[smem_spec()] + [vmem_spec()] * 4,
        out_specs=vmem_spec(),
        out_shape=jax.ShapeDtypeStruct(ints.shape, F32),
        compiler_params=params(16),
        name="coupling",
    )(near, own, following, inter, ints)


def update_kernel(atoms, terms_ref, rest_ref, across_ref, down_ref, shift, out_ref):
    total = rest_ref[...]
    for t in range(atoms.shape[0]):
        total = total + terms_ref[atoms[t]].astype(F32)
    denominator = down_ref[...] + across_ref[...] + shift[0]
    out_ref[...] = (-total / denominator).astype(out_ref.dtype)


def update_pair(atoms, terms, rest, across, down, shift, dtype):
    return pl.pallas_call(
        update_kernel,
        in_specs=[smem_spec()] + [vmem_spec()] * 4 + [smem_spec()],
        out_specs=vmem_spec(),
        out_shape=jax.ShapeDtypeStruct(rest.shape, dtype),
        compiler_params=params(16),
        name="update",
    )(atoms, terms, rest, across, down, shift)


def on_device(
    amplitudes,
    bases,
    factors,
    intersections,
    pair_integrals,
    pno_energies,
    pair_shift,
    pair_atoms,
    pair_next,
):
    me = lax.axis_index("dev")
    count = lax.axis_size("dev")
    listed = jnp.any(pair_atoms == me, axis=1)
    order = jnp.sort(jnp.where(listed, jnp.arange(count), count))[:CAP].astype(jnp.int32)
    slots = jnp.where(order < count, order ^ me, 0)
    pairs = jnp.where(order < count, order, -1)
    atoms = pair_atoms[me]
    near = pair_next[0]
    near = jnp.where(near < count, near ^ me, ((near - count) ^ me) + count)
    across = pno_energies
    down = pno_energies.reshape(-1, 1)
    inter = intersections[0]
    ints = pair_integrals[0]

    group_bases = gather_near(gather_across(bases, "dev"), "dev")
    pair_amps, group_bases[1] = lax.optimization_barrier(
        (gather_across(amplitudes, "dev"), group_bases[1])
    )
    group_amps = gather_near(pair_amps, "dev")
    projected = project(slots, group_bases, factors[0])
    for iteration in range(ITERS):
        stacked = jnp.concatenate(
            [g[r : r + 1] for r in range(2) for g in group_amps], axis=0
        )
        following = from_next(stacked, "grp")
        terms = ladder(count, slots, pairs, group_amps, projected)
        terms, following = lax.optimization_barrier((terms, following))
        arrived = lax.all_to_all(terms, "dev", split_axis=0, concat_axis=0, tiled=True)
        rest = coupling(near, stacked, following, inter, ints)
        last = iteration + 1 == ITERS
        update = update_pair(
            atoms, arrived, rest, across, down, pair_shift, F32 if last else BF16
        )
        if not last:
            group_amps = gather_near(gather_across(update[None], "dev"), "dev")
    return update[None]


def solution(mesh):
    return jax.shard_map(
        on_device,
        mesh=mesh,
        in_specs=(
            P(("grp", "dev"), None, None),
            P(("grp", "dev"), None, None),
            P(("grp", "dev"), None, None, None),
            P(("grp", "dev"), None, None, None),
            P(("grp", "dev"), None, None),
            P(("grp", "dev"), None),
            P(("grp", "dev")),
            P("grp", None),
            P(("grp", "dev"), None),
        ),
        out_specs=P(("grp", "dev"), None, None),
        check_vma=False,
    )
```

profile of v0, /device:TPU:1, one launch (start us, length us, event | category | flops | bytes accessed | tf_op | source)
XLA Modules:
  0.0 83.7 jit_solution(8804583587643565875)
XLA Ops:
  0.0 3.1 %collective-permute-start = (bf16[1,128,128]{2,1,0:T(8,128)(2,1)}, bf16[1,128,128]{2,1,0:T(8,128)(2,1)S(1)}, u32[]{:S(2)}, u32[]{:S(2)}) collective-permute-start(bf16[1,128,128]{2,1,0:T(8,128)(2,1)} %param.9), channel_id=1, source_target_pairs={{0,4},{1,5},{2,6},{3,7},{4,0},{5,1},{6,2},{7,3},{8,12},{9,13},{10,... | collective-permute-start | bytes 98312 | tf_op jit(solution)/shard_map/ppermute | solution.py:28
  4.8 2.8 %collective-permute-done.1 = bf16[1,256,128]{2,1,0:T(8,128)(2,1)S(1)} collective-permute-done((bf16[1,256,128]{2,1,0:T(8,128)(2,1)}, bf16[1,256,128]{2,1,0:T(8,128)(2,1)S(1)}, u32[]{:S(2)}, u32[]{:S(2)}) %collective-permute-start.1) | collective-permute-done | bytes 65568 | tf_op jit(solution)/shard_map/ppermute | solution.py:28
  7.6 1.3 %collective-permute-start.2 = (bf16[2,256,128]{2,1,0:T(8,128)(2,1)S(1)}, bf16[2,256,128]{2,1,0:T(8,128)(2,1)S(1)}, u32[]{:S(2)}, u32[]{:S(2)}) collective-permute-start(bf16[2,256,128]{2,1,0:T(8,128)(2,1)S(1)} %constant_dynamic-update-slice_fusion.refs_1_), channel_id=1, source_target_pairs={{0,1},{1,0},{2,3},{3,2},{4,5},{5,4},{6,7},{7,6},{8,9},{9,8},{10,11... | collective-permute-start | bytes 393224 | tf_op jit(solution)/shard_map/ppermute | solution.py:28
  8.9 1.0 %sort.15 = (s32[8]{0:T(128)S(1)}, s32[8]{0:T(128)}) sort(s32[8]{0:T(128)S(1)} %iota_select_fusion, s32[8]{0:T(128)S(1)} %iota.7), dimensions={0}, to_apply=%region_1.2 | sort | flops 24 | bytes 128 | tf_op jit(solution)/shard_map/jit(sort)/sort | solution.py:240
  10.6 1.7 %collective-permute-start.6 = (bf16[2,256,128]{2,1,0:T(8,128)(2,1)S(1)}, bf16[2,256,128]{2,1,0:T(8,128)(2,1)S(1)}, u32[]{:S(2)}, u32[]{:S(2)}) collective-permute-start(bf16[2,256,128]{2,1,0:T(8,128)(2,1)S(1)} %constant_dynamic-update-slice_fusion.refs_1_), channel_id=1, source_target_pairs={{0,2},{1,3},{2,0},{3,1},{4,6},{5,7},{6,4},{7,5},{8,10},{9,11},{10,... | collective-permute-start | bytes 393224 | tf_op jit(solution)/shard_map/ppermute | solution.py:28
  12.3 1.2 %collective-permute-start.3 = (bf16[2,128,128]{2,1,0:T(8,128)(2,1)S(1)}, bf16[2,128,128]{2,1,0:T(8,128)(2,1)S(1)}, u32[]{:S(2)}, u32[]{:S(2)}) collective-permute-start(bf16[2,128,128]{2,1,0:T(8,128)(2,1)S(1)} %pad_maximum_fusion.refs_2_), channel_id=1, source_target_pairs={{0,1},{1,0},{2,3},{3,2},{4,5},{5,4},{6,7},{7,6},{8,9},{9,8},{10,11... | collective-permute-start | bytes 196616 | tf_op jit(solution)/shard_map/ppermute | solution.py:28
  13.6 1.4 %collective-permute-start.4 = (bf16[2,128,128]{2,1,0:T(8,128)(2,1)S(1)}, bf16[2,128,128]{2,1,0:T(8,128)(2,1)S(1)}, u32[]{:S(2)}, u32[]{:S(2)}) collective-permute-start(bf16[2,128,128]{2,1,0:T(8,128)(2,1)S(1)} %pad_maximum_fusion.refs_2_), channel_id=1, source_target_pairs={{0,2},{1,3},{2,0},{3,1},{4,6},{5,7},{6,4},{7,5},{8,10},{9,11},{10,... | collective-permute-start | bytes 196616 | tf_op jit(solution)/shard_map/ppermute | solution.py:28
  15.0 1.1 %collective-permute-done.3.refs_3_ = bf16[2,128,128]{2,1,0:T(8,128)(2,1)S(1)} collective-permute-done((bf16[2,128,128]{2,1,0:T(8,128)(2,1)S(1)}, bf16[2,128,128]{2,1,0:T(8,128)(2,1)S(1)}, u32[]{:S(2)}, u32[]{:S(2)}) %collective-permute-start.3) | collective-permute-done | bytes 65568 | tf_op jit(solution)/shard_map/ppermute | solution.py:28
  16.1 1.8 %collective-permute-done.4.refs_4_ = bf16[2,128,128]{2,1,0:T(8,128)(2,1)S(1)} collective-permute-done((bf16[2,128,128]{2,1,0:T(8,128)(2,1)S(1)}, bf16[2,128,128]{2,1,0:T(8,128)(2,1)S(1)}, u32[]{:S(2)}, u32[]{:S(2)}) %collective-permute-start.4) | collective-permute-done | bytes 65568 | tf_op jit(solution)/shard_map/ppermute | solution.py:28
  17.8 3.4 %collective-permute-done.5.refs_5_ = bf16[2,128,128]{2,1,0:T(8,128)(2,1)S(1)} collective-permute-done((bf16[2,128,128]{2,1,0:T(8,128)(2,1)S(1)}, bf16[2,128,128]{2,1,0:T(8,128)(2,1)S(1)}, u32[]{:S(2)}, u32[]{:S(2)}) %collective-permute-start.5) | collective-permute-done | bytes 65568 | tf_op jit(solution)/shard_map/ppermute | solution.py:28
  21.3 4.0 %collective-permute-start.8 = (bf16[8,128,128]{2,1,0:T(8,128)(2,1)S(1)}, bf16[8,128,128]{2,1,0:T(8,128)(2,1)S(1)}, u32[]{:S(2)}, u32[]{:S(2)}) collective-permute-start(bf16[8,128,128]{2,1,0:T(8,128)(2,1)S(1)} %constant_dynamic-update-slice_fusion.2.own_ref), channel_id=1, source_target_pairs={{8,0},{16,8},{24,16},{9,1},{17,9},{25,17},{10,2},{18,10},{26,18},{... | collective-permute-start | bytes 786440 | tf_op jit(solution)/shard_map/ppermute | solution.py:43
  25.4 6.1 %project.1.refs_6_ = bf16[3,16,128,256]{3,2,1,0:T(8,128)(2,1)S(1)} custom-call(s32[3]{0:T(128)S(1)} %get-tuple-element.21.refs_0_, bf16[2,256,128]{2,1,0:T(8,128)(2,1)S(1)} %constant_dynamic-update-slice_fusion.refs_1_, bf16[2,256,128]{2,1,0:T(8,128)(2,1)S(1)} %collective-permute-done.2.refs_2_, bf16[2,256,128]{2,1,0:T(8,128)(2,1)S(1)} %collective-permute-done.6.refs_3_, ...), custom_call_target="tpu_custom_call" | custom-call | flops 2415919104 | bytes 4194304 | tf_op jit(solution)/shard_map/project/pallas_call | solution.py:80
  31.5 3.5 %ladder.2 = bf16[8,128,128]{2,1,0:T(8,128)(2,1)S(1)} custom-call(s32[3]{0:T(128)S(1)} %get-tuple-element.21.refs_0_, s32[3]{0:T(128)S(1)} %get-tuple-element.20.refs_1_, bf16[2,128,128]{2,1,0:T(8,128)(2,1)S(1)} %pad_maximum_fusion.refs_2_, bf16[2,128,128]{2,1,0:T(8,128)(2,1)S(1)} %collective-permute-done.3.refs_3_, ...), custom_call_target="tpu_custom_call" | custom-call | bytes 12582912 | tf_op jit(solution)/shard_map/ladder/pallas_call | solution.py:156
  36.4 5.4 %all-to-all-start = ((bf16[8,128,128]{2,1,0:T(8,128)(2,1)}), bf16[8,128,128]{2,1,0:T(8,128)(2,1)S(1)}, u32[]{:S(2)}, u32[]{:S(2)}) async-start(bf16[8,128,128]{2,1,0:T(8,128)(2,1)} %copy-done), calls=%async_computation | async-start | bytes 524288 | tf_op jit(solution)/shard_map/all_to_all | solution.py:264
  44.2 0.9 %copy-done.6 = bf16[8,128,128]{2,1,0:T(8,128)(2,1)S(1)} copy-done((bf16[8,128,128]{2,1,0:T(8,128)(2,1)S(1)}, bf16[8,128,128]{2,1,0:T(8,128)(2,1)}, u32[]{:S(2)}) %copy-start.6) | copy-done | bytes 262168
  45.1 0.9 %copy-done.8 = bf16[8,128,128]{2,1,0:T(8,128)(2,1)S(1)} copy-done((bf16[8,128,128]{2,1,0:T(8,128)(2,1)S(1)}, bf16[8,128,128]{2,1,0:T(8,128)(2,1)}, u32[]{:S(2)}) %copy-start.8) | copy-done | bytes 262168
  46.9 1.0 %coupling.2.rest_ref = f32[128,128]{1,0:T(8,128)S(1)} custom-call(s32[4]{0:T(128)S(1)} %fusion.near, bf16[8,128,128]{2,1,0:T(8,128)(2,1)S(1)} %copy-done.6, bf16[8,128,128]{2,1,0:T(8,128)(2,1)S(1)} %copy-done.8, bf16[4,128,128]{2,1,0:T(8,128)(2,1)S(1)} %bitcast.9, f32[128,128]{1,0:T(8,128)S(1)} %bitcast.13), custom_call_target="tpu_custom_call" | custom-call | tf_op jit(solution)/shard_map/coupling/pallas_call | solution.py:197
  47.9 3.1 %all-to-all-done.terms_ref = bf16[8,128,128]{2,1,0:T(8,128)(2,1)S(1)} async-done(((bf16[8,128,128]{2,1,0:T(8,128)(2,1)}), bf16[8,128,128]{2,1,0:T(8,128)(2,1)S(1)}, u32[]{:S(2)}, u32[]{:S(2)}) %all-to-all-start) | async-done | bytes 262176 | tf_op jit(solution)/shard_map/all_to_all | solution.py:264
  52.4 3.1 %collective-permute-done.9 = bf16[1,128,128]{2,1,0:T(8,128)(2,1)S(1)} collective-permute-done((bf16[1,128,128]{2,1,0:T(8,128)(2,1)S(1)}, bf16[1,128,128]{2,1,0:T(8,128)(2,1)S(1)}, u32[]{:S(2)}, u32[]{:S(2)}) %collective-permute-start.9) | collective-permute-done | bytes 32800 | tf_op jit(solution)/shard_map/ppermute | solution.py:28
  55.5 1.2 %collective-permute-start.10 = (bf16[2,128,128]{2,1,0:T(8,128)(2,1)S(1)}, bf16[2,128,128]{2,1,0:T(8,128)(2,1)S(1)}, u32[]{:S(2)}, u32[]{:S(2)}) collective-permute-start(bf16[2,128,128]{2,1,0:T(8,128)(2,1)S(1)} %pad_maximum_fusion.1.refs_2_), channel_id=1, source_target_pairs={{0,1},{1,0},{2,3},{3,2},{4,5},{5,4},{6,7},{7,6},{8,9},{9,8},{10,11... | collective-permute-start | bytes 196616 | tf_op jit(solution)/shard_map/ppermute | solution.py:28
  56.7 1.5 %collective-permute-start.12 = (bf16[2,128,128]{2,1,0:T(8,128)(2,1)S(1)}, bf16[2,128,128]{2,1,0:T(8,128)(2,1)S(1)}, u32[]{:S(2)}, u32[]{:S(2)}) collective-permute-start(bf16[2,128,128]{2,1,0:T(8,128)(2,1)S(1)} %pad_maximum_fusion.1.refs_2_), channel_id=1, source_target_pairs={{0,3},{1,2},{2,1},{3,0},{4,7},{5,6},{6,5},{7,4},{8,11},{9,10},{10,... | collective-permute-start | bytes 196616 | tf_op jit(solution)/shard_map/ppermute | solution.py:28
  58.7 1.2 %collective-permute-done.11.refs_4_ = bf16[2,128,128]{2,1,0:T(8,128)(2,1)S(1)} collective-permute-done((bf16[2,128,128]{2,1,0:T(8,128)(2,1)S(1)}, bf16[2,128,128]{2,1,0:T(8,128)(2,1)S(1)}, u32[]{:S(2)}, u32[]{:S(2)}) %collective-permute-start.11) | collective-permute-done | bytes 65568 | tf_op jit(solution)/shard_map/ppermute | solution.py:28
  59.9 1.0 %collective-permute-done.12.refs_5_ = bf16[2,128,128]{2,1,0:T(8,128)(2,1)S(1)} collective-permute-done((bf16[2,128,128]{2,1,0:T(8,128)(2,1)S(1)}, bf16[2,128,128]{2,1,0:T(8,128)(2,1)S(1)}, u32[]{:S(2)}, u32[]{:S(2)}) %collective-permute-start.12) | collective-permute-done | bytes 65568 | tf_op jit(solution)/shard_map/ppermute | solution.py:28
  60.9 5.1 %collective-permute-start.13 = (bf16[8,128,128]{2,1,0:T(8,128)(2,1)S(1)}, bf16[8,128,128]{2,1,0:T(8,128)(2,1)S(1)}, u32[]{:S(2)}, u32[]{:S(2)}) collective-permute-start(bf16[8,128,128]{2,1,0:T(8,128)(2,1)S(1)} %constant_dynamic-update-slice_fusion.10.own_ref), channel_id=1, source_target_pairs={{8,0},{16,8},{24,16},{9,1},{17,9},{25,17},{10,2},{18,10},{26,18},{... | collective-permute-start | bytes 786440 | tf_op jit(solution)/shard_map/ppermute | solution.py:43
  66.0 3.4 %ladder.3 = bf16[8,128,128]{2,1,0:T(8,128)(2,1)} custom-call(s32[3]{0:T(128)S(1)} %get-tuple-element.21.refs_0_, s32[3]{0:T(128)S(1)} %get-tuple-element.20.refs_1_, bf16[2,128,128]{2,1,0:T(8,128)(2,1)S(1)} %pad_maximum_fusion.1.refs_2_, bf16[2,128,128]{2,1,0:T(8,128)(2,1)S(1)} %collective-permute-done.10.refs_3_, ...), custom_call_target="tpu_custom_call" | custom-call | bytes 12582912 | tf_op jit(solution)/shard_map/ladder/pallas_call | solution.py:156
  69.4 1.7 %collective-permute-done.13.next_ref = bf16[8,128,128]{2,1,0:T(8,128)(2,1)S(1)} collective-permute-done((bf16[8,128,128]{2,1,0:T(8,128)(2,1)S(1)}, bf16[8,128,128]{2,1,0:T(8,128)(2,1)S(1)}, u32[]{:S(2)}, u32[]{:S(2)}) %collective-permute-start.13) | collective-permute-done | bytes 262176 | tf_op jit(solution)/shard_map/ppermute | solution.py:43
  71.7 3.4 %all-to-all-start.1 = ((bf16[8,128,128]{2,1,0:T(8,128)(2,1)}), bf16[8,128,128]{2,1,0:T(8,128)(2,1)S(1)}, u32[]{:S(2)}, u32[]{:S(2)}) async-start(bf16[8,128,128]{2,1,0:T(8,128)(2,1)} %ladder.3), calls=%async_computation.1 | async-start | bytes 524288 | tf_op jit(solution)/shard_map/all_to_all | solution.py:264
  75.2 0.9 %copy-done.4 = bf16[8,128,128]{2,1,0:T(8,128)(2,1)S(1)} copy-done((bf16[8,128,128]{2,1,0:T(8,128)(2,1)S(1)}, bf16[8,128,128]{2,1,0:T(8,128)(2,1)}, u32[]{:S(2)}) %copy-start.4) | copy-done | bytes 262168
  76.2 0.9 %copy-done.10 = bf16[8,128,128]{2,1,0:T(8,128)(2,1)S(1)} copy-done((bf16[8,128,128]{2,1,0:T(8,128)(2,1)S(1)}, bf16[8,128,128]{2,1,0:T(8,128)(2,1)}, u32[]{:S(2)}) %copy-start.10) | copy-done | bytes 262168
  77.1 1.0 %coupling.3.rest_ref = f32[128,128]{1,0:T(8,128)S(1)} custom-call(s32[4]{0:T(128)S(1)} %copy-done.15, bf16[8,128,128]{2,1,0:T(8,128)(2,1)S(1)} %copy-done.4, bf16[8,128,128]{2,1,0:T(8,128)(2,1)S(1)} %copy-done.10, bf16[4,128,128]{2,1,0:T(8,128)(2,1)S(1)} %bitcast.10, f32[128,128]{1,0:T(8,128)S(1)} %bitcast.14), custom_call_target="tpu_custom_call" | custom-call | tf_op jit(solution)/shard_map/coupling/pallas_call | solution.py:197
  78.1 4.3 %all-to-all-done.1.terms_ref = bf16[8,128,128]{2,1,0:T(8,128)(2,1)S(1)} async-done(((bf16[8,128,128]{2,1,0:T(8,128)(2,1)}), bf16[8,128,128]{2,1,0:T(8,128)(2,1)S(1)}, u32[]{:S(2)}, u32[]{:S(2)}) %all-to-all-start.1) | async-done | bytes 262176 | tf_op jit(solution)/shard_map/all_to_all | solution.py:264
  82.5 1.3 %update.3 = f32[128,128]{1,0:T(8,128)} custom-call(s32[2]{0:T(128)S(1)} %dynamic-slice_reduce_fusion.atoms, bf16[8,128,128]{2,1,0:T(8,128)(2,1)S(1)} %all-to-all-done.1.terms_ref, f32[128,128]{1,0:T(8,128)S(1)} %coupling.3.rest_ref, f32[1,128]{1,0:T(1,128)S(1)} %copy-done.13, f32[128,1]{1,0:T(8,128)S(1)} %copy.10.down_ref, f32[1]{0:T(128)S(6)} %copy.27.shift), custom_call_target="tpu_custom_call" | custom-call | tf_op jit(solution)/shard_map/update/pallas_call | solution.py:216
  (71 shorter events, 9.0 us)
Async XLA Ops:
  0.0 9.8 %collective-permute-start = (bf16[1,128,128]{2,1,0:T(8,128)(2,1)}, bf16[1,128,128]{2,1,0:T(8,128)(2,1)S(1)}, u32[]{:S(2)}, u32[]{:S(2)}) collective-permute-start(bf16[1,128,128]{2,1,0:T(8,128)(2,1)} %param.9), channel_id=1, source_target_pairs={{0,4},{1,5},{2,6},{3,7},{4,0},{5,1},{6,2},{7,3},{8,12},{9,13},{10,... | collective-permute-start | bytes 98312 | tf_op jit(solution)/shard_map/ppermute | solution.py:28
  3.1 4.4 %collective-permute-start.1 = (bf16[1,256,128]{2,1,0:T(8,128)(2,1)}, bf16[1,256,128]{2,1,0:T(8,128)(2,1)S(1)}, u32[]{:S(2)}, u32[]{:S(2)}) collective-permute-start(bf16[1,256,128]{2,1,0:T(8,128)(2,1)} %param.10), channel_id=1, source_target_pairs={{0,4},{1,5},{2,6},{3,7},{4,0},{5,1},{6,2},{7,3},{8,12},{9,13},{10,... | collective-permute-start | bytes 196616 | tf_op jit(solution)/shard_map/ppermute | solution.py:28
  7.6 4.8 %collective-permute-start.2 = (bf16[2,256,128]{2,1,0:T(8,128)(2,1)S(1)}, bf16[2,256,128]{2,1,0:T(8,128)(2,1)S(1)}, u32[]{:S(2)}, u32[]{:S(2)}) collective-permute-start(bf16[2,256,128]{2,1,0:T(8,128)(2,1)S(1)} %constant_dynamic-update-slice_fusion.refs_1_), channel_id=1, source_target_pairs={{0,1},{1,0},{2,3},{3,2},{4,5},{5,4},{6,7},{7,6},{8,9},{9,8},{10,11... | collective-permute-start | bytes 393224 | tf_op jit(solution)/shard_map/ppermute | solution.py:28
  10.6 14.7 %collective-permute-start.6 = (bf16[2,256,128]{2,1,0:T(8,128)(2,1)S(1)}, bf16[2,256,128]{2,1,0:T(8,128)(2,1)S(1)}, u32[]{:S(2)}, u32[]{:S(2)}) collective-permute-start(bf16[2,256,128]{2,1,0:T(8,128)(2,1)S(1)} %constant_dynamic-update-slice_fusion.refs_1_), channel_id=1, source_target_pairs={{0,2},{1,3},{2,0},{3,1},{4,6},{5,7},{6,4},{7,5},{8,10},{9,11},{10,... | collective-permute-start | bytes 393224 | tf_op jit(solution)/shard_map/ppermute | solution.py:28
  12.3 13.0 %collective-permute-start.7 = (bf16[2,256,128]{2,1,0:T(8,128)(2,1)S(1)}, bf16[2,256,128]{2,1,0:T(8,128)(2,1)S(1)}, u32[]{:S(2)}, u32[]{:S(2)}) collective-permute-start(bf16[2,256,128]{2,1,0:T(8,128)(2,1)S(1)} %constant_dynamic-update-slice_fusion.refs_1_), channel_id=1, source_target_pairs={{0,3},{1,2},{2,1},{3,0},{4,7},{5,6},{6,5},{7,4},{8,11},{9,10},{10,... | collective-permute-start | bytes 393224 | tf_op jit(solution)/shard_map/ppermute | solution.py:28
  12.3 3.7 %collective-permute-start.3 = (bf16[2,128,128]{2,1,0:T(8,128)(2,1)S(1)}, bf16[2,128,128]{2,1,0:T(8,128)(2,1)S(1)}, u32[]{:S(2)}, u32[]{:S(2)}) collective-permute-start(bf16[2,128,128]{2,1,0:T(8,128)(2,1)S(1)} %pad_maximum_fusion.refs_2_), channel_id=1, source_target_pairs={{0,1},{1,0},{2,3},{3,2},{4,5},{5,4},{6,7},{7,6},{8,9},{9,8},{10,11... | collective-permute-start | bytes 196616 | tf_op jit(solution)/shard_map/ppermute | solution.py:28
  13.6 4.3 %collective-permute-start.4 = (bf16[2,128,128]{2,1,0:T(8,128)(2,1)S(1)}, bf16[2,128,128]{2,1,0:T(8,128)(2,1)S(1)}, u32[]{:S(2)}, u32[]{:S(2)}) collective-permute-start(bf16[2,128,128]{2,1,0:T(8,128)(2,1)S(1)} %pad_maximum_fusion.refs_2_), channel_id=1, source_target_pairs={{0,2},{1,3},{2,0},{3,1},{4,6},{5,7},{6,4},{7,5},{8,10},{9,11},{10,... | collective-permute-start | bytes 196616 | tf_op jit(solution)/shard_map/ppermute | solution.py:28
  15.0 6.3 %collective-permute-start.5 = (bf16[2,128,128]{2,1,0:T(8,128)(2,1)S(1)}, bf16[2,128,128]{2,1,0:T(8,128)(2,1)S(1)}, u32[]{:S(2)}, u32[]{:S(2)}) collective-permute-start(bf16[2,128,128]{2,1,0:T(8,128)(2,1)S(1)} %pad_maximum_fusion.refs_2_), channel_id=1, source_target_pairs={{0,3},{1,2},{2,1},{3,0},{4,7},{5,6},{6,5},{7,4},{8,11},{9,10},{10,... | collective-permute-start | bytes 196616 | tf_op jit(solution)/shard_map/ppermute | solution.py:28
  21.3 10.2 %copy-start.5 = (bf16[8,128,128]{2,1,0:T(8,128)(2,1)}, bf16[8,128,128]{2,1,0:T(8,128)(2,1)S(1)}, u32[]{:S(2)}) copy-start(bf16[8,128,128]{2,1,0:T(8,128)(2,1)S(1)} %constant_dynamic-update-slice_fusion.2.own_ref) | copy-start | bytes 786436
  21.3 14.4 %collective-permute-start.8 = (bf16[8,128,128]{2,1,0:T(8,128)(2,1)S(1)}, bf16[8,128,128]{2,1,0:T(8,128)(2,1)S(1)}, u32[]{:S(2)}, u32[]{:S(2)}) collective-permute-start(bf16[8,128,128]{2,1,0:T(8,128)(2,1)S(1)} %constant_dynamic-update-slice_fusion.2.own_ref), channel_id=1, source_target_pairs={{8,0},{16,8},{24,16},{9,1},{17,9},{25,17},{10,2},{18,10},{26,18},{... | collective-permute-start | bytes 786440 | tf_op jit(solution)/shard_map/ppermute | solution.py:43
  31.5 10.3 %copy-start.16 = (s32[8,2]{0,1:T(2,128)S(1)}, s32[8,2]{0,1:T(2,128)}, u32[]{:S(2)}) copy-start(s32[8,2]{0,1:T(2,128)} %param.16) | copy-start | bytes 196
  31.5 10.5 %copy-start.13 = (f32[1,128]{1,0:T(1,128)S(1)}, f32[1,128]{1,0:T(1,128)}, u32[]{:S(2)}) copy-start(f32[1,128]{1,0:T(1,128)} %across_ref.3) | copy-start | bytes 1540
  31.5 11.2 %copy-start.17 = (s32[1,4]{1,0:T(1,128)S(1)}, s32[1,4]{1,0:T(1,128)}, u32[]{:S(2)}) copy-start(s32[1,4]{1,0:T(1,128)} %param.17) | copy-start | bytes 52
  35.0 0.7 copy-start
  35.7 0.7 copy-start.7
  36.4 14.7 %all-to-all-start = ((bf16[8,128,128]{2,1,0:T(8,128)(2,1)}), bf16[8,128,128]{2,1,0:T(8,128)(2,1)S(1)}, u32[]{:S(2)}, u32[]{:S(2)}) async-start(bf16[8,128,128]{2,1,0:T(8,128)(2,1)} %copy-done), calls=%async_computation | async-start | bytes 524288 | tf_op jit(solution)/shard_map/all_to_all | solution.py:264
  43.3 0.9 %copy-start.1 = (bf16[1,4,128,128]{3,2,1,0:T(8,128)(2,1)S(1)}, bf16[1,4,128,128]{3,2,1,0:T(8,128)(2,1)}, u32[]{:S(2)}) copy-start(bf16[1,4,128,128]{3,2,1,0:T(8,128)(2,1)} %param.12) | copy-start | bytes 393220
  44.2 0.9 %copy-start.6 = (bf16[8,128,128]{2,1,0:T(8,128)(2,1)S(1)}, bf16[8,128,128]{2,1,0:T(8,128)(2,1)}, u32[]{:S(2)}) copy-start(bf16[8,128,128]{2,1,0:T(8,128)(2,1)} %copy-done.5) | copy-start | bytes 786436
  45.1 0.9 %copy-start.8 = (bf16[8,128,128]{2,1,0:T(8,128)(2,1)S(1)}, bf16[8,128,128]{2,1,0:T(8,128)(2,1)}, u32[]{:S(2)}) copy-start(bf16[8,128,128]{2,1,0:T(8,128)(2,1)} %copy-done.7) | copy-start | bytes 786436
  46.1 0.8 %copy-start.11 = (f32[1,128,128]{2,1,0:T(8,128)S(1)}, f32[1,128,128]{2,1,0:T(8,128)}, u32[]{:S(2)}) copy-start(f32[1,128,128]{2,1,0:T(8,128)} %param.13) | copy-start | bytes 196612
  51.7 23.5 %copy-start.2 = (bf16[1,4,128,128]{3,2,1,0:T(8,128)(2,1)S(1)}, bf16[1,4,128,128]{3,2,1,0:T(8,128)(2,1)}, u32[]{:S(2)}) copy-start(bf16[1,4,128,128]{3,2,1,0:T(8,128)(2,1)} %param.12) | copy-start | bytes 393220
  51.7 23.5 %copy-start.12 = (f32[1,128,128]{2,1,0:T(8,128)S(1)}, f32[1,128,128]{2,1,0:T(8,128)}, u32[]{:S(2)}) copy-start(f32[1,128,128]{2,1,0:T(8,128)} %param.13) | copy-start | bytes 196612
  51.7 23.5 %copy-start.15 = (s32[4]{0:T(128)S(1)}, s32[4]{0:T(128)}, u32[]{:S(2)}) copy-start(s32[4]{0:T(128)} %copy-done.14) | copy-start | bytes 52
  51.7 3.7 %collective-permute-start.9 = (bf16[1,128,128]{2,1,0:T(8,128)(2,1)S(1)}, bf16[1,128,128]{2,1,0:T(8,128)(2,1)S(1)}, u32[]{:S(2)}, u32[]{:S(2)}) collective-permute-start(bf16[1,128,128]{2,1,0:T(8,128)(2,1)S(1)} %bitcast.11), channel_id=1, source_target_pairs={{0,4},{1,5},{2,6},{3,7},{4,0},{5,1},{6,2},{7,3},{8,12},{9,13},{10,... | collective-permute-start | bytes 98312 | tf_op jit(solution)/shard_map/ppermute | solution.py:28
  55.5 3.2 %collective-permute-start.10 = (bf16[2,128,128]{2,1,0:T(8,128)(2,1)S(1)}, bf16[2,128,128]{2,1,0:T(8,128)(2,1)S(1)}, u32[]{:S(2)}, u32[]{:S(2)}) collective-permute-start(bf16[2,128,128]{2,1,0:T(8,128)(2,1)S(1)} %pad_maximum_fusion.1.refs_2_), channel_id=1, source_target_pairs={{0,1},{1,0},{2,3},{3,2},{4,5},{5,4},{6,7},{7,6},{8,9},{9,8},{10,11... | collective-permute-start | bytes 196616 | tf_op jit(solution)/shard_map/ppermute | solution.py:28
  56.7 3.1 %collective-permute-start.11 = (bf16[2,128,128]{2,1,0:T(8,128)(2,1)S(1)}, bf16[2,128,128]{2,1,0:T(8,128)(2,1)S(1)}, u32[]{:S(2)}, u32[]{:S(2)}) collective-permute-start(bf16[2,128,128]{2,1,0:T(8,128)(2,1)S(1)} %pad_maximum_fusion.1.refs_2_), channel_id=1, source_target_pairs={{0,2},{1,3},{2,0},{3,1},{4,6},{5,7},{6,4},{7,5},{8,10},{9,11},{10,... | collective-permute-start | bytes 196616 | tf_op jit(solution)/shard_map/ppermute | solution.py:28
  56.7 4.1 %collective-permute-start.12 = (bf16[2,128,128]{2,1,0:T(8,128)(2,1)S(1)}, bf16[2,128,128]{2,1,0:T(8,128)(2,1)S(1)}, u32[]{:S(2)}, u32[]{:S(2)}) collective-permute-start(bf16[2,128,128]{2,1,0:T(8,128)(2,1)S(1)} %pad_maximum_fusion.1.refs_2_), channel_id=1, source_target_pairs={{0,3},{1,2},{2,1},{3,0},{4,7},{5,6},{6,5},{7,4},{8,11},{9,10},{10,... | collective-permute-start | bytes 196616 | tf_op jit(solution)/shard_map/ppermute | solution.py:28
  60.9 8.5 %copy-start.3 = (bf16[8,128,128]{2,1,0:T(8,128)(2,1)}, bf16[8,128,128]{2,1,0:T(8,128)(2,1)S(1)}, u32[]{:S(2)}) copy-start(bf16[8,128,128]{2,1,0:T(8,128)(2,1)S(1)} %constant_dynamic-update-slice_fusion.10.own_ref) | copy-start | bytes 786436
  60.9 10.2 %collective-permute-start.13 = (bf16[8,128,128]{2,1,0:T(8,128)(2,1)S(1)}, bf16[8,128,128]{2,1,0:T(8,128)(2,1)S(1)}, u32[]{:S(2)}, u32[]{:S(2)}) collective-permute-start(bf16[8,128,128]{2,1,0:T(8,128)(2,1)S(1)} %constant_dynamic-update-slice_fusion.10.own_ref), channel_id=1, source_target_pairs={{8,0},{16,8},{24,16},{9,1},{17,9},{25,17},{10,2},{18,10},{26,18},{... | collective-permute-start | bytes 786440 | tf_op jit(solution)/shard_map/ppermute | solution.py:43
  71.7 10.7 %all-to-all-start.1 = ((bf16[8,128,128]{2,1,0:T(8,128)(2,1)}), bf16[8,128,128]{2,1,0:T(8,128)(2,1)S(1)}, u32[]{:S(2)}, u32[]{:S(2)}) async-start(bf16[8,128,128]{2,1,0:T(8,128)(2,1)} %ladder.3), calls=%async_computation.1 | async-start | bytes 524288 | tf_op jit(solution)/shard_map/all_to_all | solution.py:264
  75.2 1.0 %copy-start.4 = (bf16[8,128,128]{2,1,0:T(8,128)(2,1)S(1)}, bf16[8,128,128]{2,1,0:T(8,128)(2,1)}, u32[]{:S(2)}) copy-start(bf16[8,128,128]{2,1,0:T(8,128)(2,1)} %copy-done.3) | copy-start | bytes 786436
  76.1 0.9 %copy-start.10 = (bf16[8,128,128]{2,1,0:T(8,128)(2,1)S(1)}, bf16[8,128,128]{2,1,0:T(8,128)(2,1)}, u32[]{:S(2)}) copy-start(bf16[8,128,128]{2,1,0:T(8,128)(2,1)} %copy-done.9) | copy-start | bytes 786436
  (2 other events, 1.2 us)
where the time goes:
time: 84.8 us; the launch traced here: 83.7 us
  starting transfers between devices  30.1 us (35%)
  waiting for transfers between devices  23.9 us (28%)
  Pallas kernels  16.8 us (20%)
  local copies, waits for them, and re-layouts  9.49 us (11%)
  other arithmetic  2.45 us (3%)
  between operations  0.95 us (1%)
    ppermute x12, waiting for transfers between devices, exchange(): return lax.ppermute(value, axis, [(d, d ^ offset) for d in range(count)])  14.7 us
    ppermute x12, starting transfers between devices, exchange(): return lax.ppermute(value, axis, [(d, d ^ offset) for d in range(count)])  12.2 us
    unnamed x51, local copies, waits for them, and re-layouts  9.16 us
    ppermute x2, starting transfers between devices, from_next(): return lax.ppermute(value, axis, [(d, d - 1) for d in range(1, count)])  9.1 us
    all_to_all x2, starting transfers between devices, on_device(): lax.all_to_all(terms, 'dev', split_axis=0, concat_axis=0, tiled=True)  8.8 us
    all_to_all x2, waiting for transfers between devices, on_device(): lax.all_to_all(terms, 'dev', split_axis=0, concat_axis=0, tiled=True)  7.48 us
    pallas_call x2, Pallas kernels, ladder(): pl.pallas_call(kernel, grid=(CAP,), in_specs=[smem_spec()] * 2 + [pl.Bloc...  6.83 us
    pallas_call x1, Pallas kernels, project(): pl.pallas_call(kernel, grid=(aux // step,), in_specs=[smem_spec()] + [pl....  6.09 us
  transfers between devices with their start and end apart: 16, of which 11 were waited for; matrix products, arithmetic and copies ran while one was open for 4% of the time, Pallas kernels for 18%

commit v1 on v0

--- a/solution.py
+++ b/solution.py
@@ -236,10 +236,12 @@
 ):
     me = lax.axis_index("dev")
     count = lax.axis_size("dev")
+    places = jnp.arange(count, dtype=jnp.int32)
     listed = jnp.any(pair_atoms == me, axis=1)
-    order = jnp.sort(jnp.where(listed, jnp.arange(count), count))[:CAP].astype(jnp.int32)
-    slots = jnp.where(order < count, order ^ me, 0)
-    pairs = jnp.where(order < count, order, -1)
+    rank = jnp.sum((places[None, :] < places[:, None]) & listed[None, :], axis=1)
+    chosen = listed[None, :] & (rank[None, :] == jnp.arange(CAP)[:, None])
+    pairs = jnp.sum(jnp.where(chosen, places[None, :] + 1, 0), axis=1) - 1
+    slots = jnp.where(pairs >= 0, pairs ^ me, 0)
     atoms = pair_atoms[me]
     near = pair_next[0]
     near = jnp.where(near < count, near ^ me, ((near - count) ^ me) + count)
@@ -249,11 +251,13 @@
     ints = pair_integrals[0]
 
     group_bases = gather_near(gather_across(bases, "dev"), "dev")
+    first, slots, pairs = lax.optimization_barrier((amplitudes, slots, pairs))
     pair_amps, group_bases[1] = lax.optimization_barrier(
-        (gather_across(amplitudes, "dev"), group_bases[1])
+        (gather_across(first, "dev"), group_bases[1])
     )
     group_amps = gather_near(pair_amps, "dev")
     projected = project(slots, group_bases, factors[0])
+    group_amps, projected = lax.optimization_barrier((group_amps, projected))
     for iteration in range(ITERS):
         stacked = jnp.concatenate(
             [g[r : r + 1] for r in range(2) for g in group_amps], axis=0

time: 84.8 us -> 82.1 us (0.968)
  waiting for transfers between devices: 23.9 us -> 21.8 us
    ppermute x12, waiting for transfers between devices: 14.7 us -> 12.4 us  [exchange(): return lax.ppermute(value, axis, [(d, d ^ offset) for d in range(count)])]
    ppermute x2, waiting for transfers between devices: 1.67 us -> 2.83 us  [from_next(): return lax.ppermute(value, axis, [(d, d - 1) for d in range(1, count)])]
    sort x1 -> x0, other arithmetic: 0.96 us -> none  [on_device(): jnp.sort(jnp.where(listed, jnp.arange(count), count))[:CAP]]
    all_to_all x2, waiting for transfers between devices: 7.48 us -> 6.63 us  [on_device(): lax.all_to_all(terms, 'dev', split_axis=0, concat_axis=0, tiled=True)]
  transfers between devices with their start and end apart: 16 -> 16, of which waited for: 11 -> 11; matrix products, arithmetic and copies ran while one was open for 4% -> 2% of each run, Pallas kernels for 18% -> 18%
where the time goes in v1:
time: 82.1 us; the launch traced here: 81.3 us
  starting transfers between devices  30.5 us (37%)
  waiting for transfers between devices  21.8 us (27%)
  Pallas kernels  16.8 us (20%)
  local copies, waits for them, and re-layouts  9.5 us (12%)
  other arithmetic  1.73 us (2%)
  between operations  0.98 us (1%)
    ppermute x12, starting transfers between devices, exchange(): return lax.ppermute(value, axis, [(d, d ^ offset) for d in range(count)])  12.6 us
    ppermute x12, waiting for transfers between devices, exchange(): return lax.ppermute(value, axis, [(d, d ^ offset) for d in range(count)])  12.4 us
    ppermute x2, starting transfers between devices, from_next(): return lax.ppermute(value, axis, [(d, d - 1) for d in range(1, count)])  9.47 us
    unnamed x51, local copies, waits for them, and re-layouts  9.17 us
    all_to_all x2, starting transfers between devices, on_device(): lax.all_to_all(terms, 'dev', split_axis=0, concat_axis=0, tiled=True)  8.41 us
    pallas_call x2, Pallas kernels, ladder(): pl.pallas_call(kernel, grid=(CAP,), in_specs=[smem_spec()] * 2 + [pl.Bloc...  6.83 us
    all_to_all x2, waiting for transfers between devices, on_device(): lax.all_to_all(terms, 'dev', split_axis=0, concat_axis=0, tiled=True)  6.63 us
    pallas_call x1, Pallas kernels, project(): pl.pallas_call(kernel, grid=(aux // step,), in_specs=[smem_spec()] + [pl....  6.07 us
  transfers between devices with their start and end apart: 16, of which 11 were waited for; matrix products, arithmetic and copies ran while one was open for 2% of the time, Pallas kernels for 18%

profile of v1, /device:TPU:1, one launch (start us, length us, event | category | flops | bytes accessed | tf_op | source)
XLA Modules:
  0.0 81.3 jit_solution(4574217682577500488)
XLA Ops:
  1.0 3.2 %collective-permute-start = (bf16[1,128,128]{2,1,0:T(8,128)(2,1)}, bf16[1,128,128]{2,1,0:T(8,128)(2,1)S(1)}, u32[]{:S(2)}, u32[]{:S(2)}) collective-permute-start(bf16[1,128,128]{2,1,0:T(8,128)(2,1)} %param.9), channel_id=1, source_target_pairs={{0,4},{1,5},{2,6},{3,7},{4,0},{5,1},{6,2},{7,3},{8,12},{9,13},{10,... | collective-permute-start | bytes 98312 | tf_op jit(solution)/shard_map/ppermute | solution.py:28
  4.2 0.9 %constant_dynamic-update-slice_fusion.1 = bf16[2,256,128]{2,1,0:T(8,128)(2,1)S(1)} fusion(bf16[1,256,128]{2,1,0:T(8,128)(2,1)} %param.10), kind=kLoop, calls=%fused_computation.3 | loop fusion | bytes 131072
  5.1 3.5 %collective-permute-done.1 = bf16[1,256,128]{2,1,0:T(8,128)(2,1)S(1)} collective-permute-done((bf16[1,256,128]{2,1,0:T(8,128)(2,1)}, bf16[1,256,128]{2,1,0:T(8,128)(2,1)S(1)}, u32[]{:S(2)}, u32[]{:S(2)}) %collective-permute-start.1) | collective-permute-done | bytes 65568 | tf_op jit(solution)/shard_map/ppermute | solution.py:28
  8.6 1.3 %collective-permute-start.2 = (bf16[2,256,128]{2,1,0:T(8,128)(2,1)S(1)}, bf16[2,256,128]{2,1,0:T(8,128)(2,1)S(1)}, u32[]{:S(2)}, u32[]{:S(2)}) collective-permute-start(bf16[2,256,128]{2,1,0:T(8,128)(2,1)S(1)} %constant_dynamic-update-slice_fusion.refs_1_), channel_id=1, source_target_pairs={{0,1},{1,0},{2,3},{3,2},{4,5},{5,4},{6,7},{7,6},{8,9},{9,8},{10,11... | collective-permute-start | bytes 393224 | tf_op jit(solution)/shard_map/ppermute | solution.py:28
  9.9 1.7 %collective-permute-start.6 = (bf16[2,256,128]{2,1,0:T(8,128)(2,1)S(1)}, bf16[2,256,128]{2,1,0:T(8,128)(2,1)S(1)}, u32[]{:S(2)}, u32[]{:S(2)}) collective-permute-start(bf16[2,256,128]{2,1,0:T(8,128)(2,1)S(1)} %constant_dynamic-update-slice_fusion.refs_1_), channel_id=1, source_target_pairs={{0,2},{1,3},{2,0},{3,1},{4,6},{5,7},{6,4},{7,5},{8,10},{9,11},{10,... | collective-permute-start | bytes 393224 | tf_op jit(solution)/shard_map/ppermute | solution.py:28
  11.6 0.8 pad_maximum_fusion.refs_2_
  12.5 1.2 %collective-permute-start.3 = (bf16[2,128,128]{2,1,0:T(8,128)(2,1)S(1)}, bf16[2,128,128]{2,1,0:T(8,128)(2,1)S(1)}, u32[]{:S(2)}, u32[]{:S(2)}) collective-permute-start(bf16[2,128,128]{2,1,0:T(8,128)(2,1)S(1)} %pad_maximum_fusion.refs_2_), channel_id=1, source_target_pairs={{0,1},{1,0},{2,3},{3,2},{4,5},{5,4},{6,7},{7,6},{8,9},{9,8},{10,11... | collective-permute-start | bytes 196616 | tf_op jit(solution)/shard_map/ppermute | solution.py:28
  13.7 1.7 %collective-permute-start.4 = (bf16[2,128,128]{2,1,0:T(8,128)(2,1)S(1)}, bf16[2,128,128]{2,1,0:T(8,128)(2,1)S(1)}, u32[]{:S(2)}, u32[]{:S(2)}) collective-permute-start(bf16[2,128,128]{2,1,0:T(8,128)(2,1)S(1)} %pad_maximum_fusion.refs_2_), channel_id=1, source_target_pairs={{0,2},{1,3},{2,0},{3,1},{4,6},{5,7},{6,4},{7,5},{8,10},{9,11},{10,... | collective-permute-start | bytes 196616 | tf_op jit(solution)/shard_map/ppermute | solution.py:28
  15.4 2.0 %collective-permute-done.7.refs_4_ = bf16[2,256,128]{2,1,0:T(8,128)(2,1)S(1)} collective-permute-done((bf16[2,256,128]{2,1,0:T(8,128)(2,1)S(1)}, bf16[2,256,128]{2,1,0:T(8,128)(2,1)S(1)}, u32[]{:S(2)}, u32[]{:S(2)}) %collective-permute-start.7) | collective-permute-done | bytes 131104 | tf_op jit(solution)/shard_map/ppermute | solution.py:28
  17.4 6.1 %project.1.refs_6_ = bf16[3,16,128,256]{3,2,1,0:T(8,128)(2,1)S(1)} custom-call(s32[3]{0:T(128)S(1)} %get-tuple-element.19.refs_0_, bf16[2,256,128]{2,1,0:T(8,128)(2,1)S(1)} %constant_dynamic-update-slice_fusion.refs_1_, bf16[2,256,128]{2,1,0:T(8,128)(2,1)S(1)} %collective-permute-done.2.refs_2_, bf16[2,256,128]{2,1,0:T(8,128)(2,1)S(1)} %collective-permute-done.6.refs_3_, ...), custom_call_target="tpu_custom_call" | custom-call | flops 2415919104 | bytes 4194304 | tf_op jit(solution)/shard_map/project/pallas_call | solution.py:80
  23.7 5.7 %collective-permute-start.8 = (bf16[8,128,128]{2,1,0:T(8,128)(2,1)S(1)}, bf16[8,128,128]{2,1,0:T(8,128)(2,1)S(1)}, u32[]{:S(2)}, u32[]{:S(2)}) collective-permute-start(bf16[8,128,128]{2,1,0:T(8,128)(2,1)S(1)} %constant_dynamic-update-slice_fusion.2.own_ref), channel_id=1, source_target_pairs={{8,0},{16,8},{24,16},{9,1},{17,9},{25,17},{10,2},{18,10},{26,18},{... | collective-permute-start | bytes 786440 | tf_op jit(solution)/shard_map/ppermute | solution.py:43
  29.4 3.5 %ladder.2 = bf16[8,128,128]{2,1,0:T(8,128)(2,1)S(1)} custom-call(s32[3]{0:T(128)S(1)} %get-tuple-element.19.refs_0_, s32[3]{0:T(128)S(1)} %get-tuple-element.20.refs_1_, bf16[2,128,128]{2,1,0:T(8,128)(2,1)S(1)} %pad_maximum_fusion.refs_2_, bf16[2,128,128]{2,1,0:T(8,128)(2,1)S(1)} %collective-permute-done.3.refs_3_, ...), custom_call_target="tpu_custom_call" | custom-call | bytes 12582912 | tf_op jit(solution)/shard_map/ladder/pallas_call | solution.py:156
  33.6 1.0 %collective-permute-done.8.next_ref = bf16[8,128,128]{2,1,0:T(8,128)(2,1)S(1)} collective-permute-done((bf16[8,128,128]{2,1,0:T(8,128)(2,1)S(1)}, bf16[8,128,128]{2,1,0:T(8,128)(2,1)S(1)}, u32[]{:S(2)}, u32[]{:S(2)}) %collective-permute-start.8) | collective-permute-done | bytes 262176 | tf_op jit(solution)/shard_map/ppermute | solution.py:43
  35.3 5.0 %all-to-all-start = ((bf16[8,128,128]{2,1,0:T(8,128)(2,1)}), bf16[8,128,128]{2,1,0:T(8,128)(2,1)S(1)}, u32[]{:S(2)}, u32[]{:S(2)}) async-start(bf16[8,128,128]{2,1,0:T(8,128)(2,1)} %copy-done), calls=%async_computation | async-start | bytes 524288 | tf_op jit(solution)/shard_map/all_to_all | solution.py:268
  41.8 0.9 %copy-done.1 = bf16[1,4,128,128]{3,2,1,0:T(8,128)(2,1)S(1)} copy-done((bf16[1,4,128,128]{3,2,1,0:T(8,128)(2,1)S(1)}, bf16[1,4,128,128]{3,2,1,0:T(8,128)(2,1)}, u32[]{:S(2)}) %copy-start.1) | copy-done | bytes 131096
  42.7 0.9 %copy-done.6 = bf16[8,128,128]{2,1,0:T(8,128)(2,1)S(1)} copy-done((bf16[8,128,128]{2,1,0:T(8,128)(2,1)S(1)}, bf16[8,128,128]{2,1,0:T(8,128)(2,1)}, u32[]{:S(2)}) %copy-start.6) | copy-done | bytes 262168
  43.6 0.9 %copy-done.8 = bf16[8,128,128]{2,1,0:T(8,128)(2,1)S(1)} copy-done((bf16[8,128,128]{2,1,0:T(8,128)(2,1)S(1)}, bf16[8,128,128]{2,1,0:T(8,128)(2,1)}, u32[]{:S(2)}) %copy-start.8) | copy-done | bytes 262168
  44.6 0.8 %copy-done.11 = f32[1,128,128]{2,1,0:T(8,128)S(1)} copy-done((f32[1,128,128]{2,1,0:T(8,128)S(1)}, f32[1,128,128]{2,1,0:T(8,128)}, u32[]{:S(2)}) %copy-start.11) | copy-done | bytes 65560
  45.4 1.0 %coupling.2.rest_ref = f32[128,128]{1,0:T(8,128)S(1)} custom-call(s32[4]{0:T(128)S(1)} %fusion.2.near, bf16[8,128,128]{2,1,0:T(8,128)(2,1)S(1)} %copy-done.6, bf16[8,128,128]{2,1,0:T(8,128)(2,1)S(1)} %copy-done.8, bf16[4,128,128]{2,1,0:T(8,128)(2,1)S(1)} %bitcast.9, f32[128,128]{1,0:T(8,128)S(1)} %bitcast.13), custom_call_target="tpu_custom_call" | custom-call | tf_op jit(solution)/shard_map/coupling/pallas_call | solution.py:197
  46.4 2.2 %all-to-all-done.terms_ref = bf16[8,128,128]{2,1,0:T(8,128)(2,1)S(1)} async-done(((bf16[8,128,128]{2,1,0:T(8,128)(2,1)}), bf16[8,128,128]{2,1,0:T(8,128)(2,1)S(1)}, u32[]{:S(2)}, u32[]{:S(2)}) %all-to-all-start) | async-done | bytes 262176 | tf_op jit(solution)/shard_map/all_to_all | solution.py:268
  50.0 4.2 %collective-permute-done.9 = bf16[1,128,128]{2,1,0:T(8,128)(2,1)S(1)} collective-permute-done((bf16[1,128,128]{2,1,0:T(8,128)(2,1)S(1)}, bf16[1,128,128]{2,1,0:T(8,128)(2,1)S(1)}, u32[]{:S(2)}, u32[]{:S(2)}) %collective-permute-start.9) | collective-permute-done | bytes 32800 | tf_op jit(solution)/shard_map/ppermute | solution.py:28
  54.4 2.5 %collective-permute-start.12 = (bf16[2,128,128]{2,1,0:T(8,128)(2,1)S(1)}, bf16[2,128,128]{2,1,0:T(8,128)(2,1)S(1)}, u32[]{:S(2)}, u32[]{:S(2)}) collective-permute-start(bf16[2,128,128]{2,1,0:T(8,128)(2,1)S(1)} %pad_maximum_fusion.1.refs_2_), channel_id=1, source_target_pairs={{0,3},{1,2},{2,1},{3,0},{4,7},{5,6},{6,5},{7,4},{8,11},{9,10},{10,... | collective-permute-start | bytes 196616 | tf_op jit(solution)/shard_map/ppermute | solution.py:28
  57.9 1.6 %collective-permute-done.12.refs_5_ = bf16[2,128,128]{2,1,0:T(8,128)(2,1)S(1)} collective-permute-done((bf16[2,128,128]{2,1,0:T(8,128)(2,1)S(1)}, bf16[2,128,128]{2,1,0:T(8,128)(2,1)S(1)}, u32[]{:S(2)}, u32[]{:S(2)}) %collective-permute-start.12) | collective-permute-done | bytes 65568 | tf_op jit(solution)/shard_map/ppermute | solution.py:28
  59.6 3.8 %collective-permute-start.13 = (bf16[8,128,128]{2,1,0:T(8,128)(2,1)S(1)}, bf16[8,128,128]{2,1,0:T(8,128)(2,1)S(1)}, u32[]{:S(2)}, u32[]{:S(2)}) collective-permute-start(bf16[8,128,128]{2,1,0:T(8,128)(2,1)S(1)} %constant_dynamic-update-slice_fusion.10.own_ref), channel_id=1, source_target_pairs={{8,0},{16,8},{24,16},{9,1},{17,9},{25,17},{10,2},{18,10},{26,18},{... | collective-permute-start | bytes 786440 | tf_op jit(solution)/shard_map/ppermute | solution.py:43
  63.3 3.4 %ladder.3 = bf16[8,128,128]{2,1,0:T(8,128)(2,1)} custom-call(s32[3]{0:T(128)S(1)} %get-tuple-element.19.refs_0_, s32[3]{0:T(128)S(1)} %get-tuple-element.20.refs_1_, bf16[2,128,128]{2,1,0:T(8,128)(2,1)S(1)} %pad_maximum_fusion.1.refs_2_, bf16[2,128,128]{2,1,0:T(8,128)(2,1)S(1)} %collective-permute-done.10.refs_3_, ...), custom_call_target="tpu_custom_call" | custom-call | bytes 12582912 | tf_op jit(solution)/shard_map/ladder/pallas_call | solution.py:156
  66.7 1.9 %collective-permute-done.13.next_ref = bf16[8,128,128]{2,1,0:T(8,128)(2,1)S(1)} collective-permute-done((bf16[8,128,128]{2,1,0:T(8,128)(2,1)S(1)}, bf16[8,128,128]{2,1,0:T(8,128)(2,1)S(1)}, u32[]{:S(2)}, u32[]{:S(2)}) %collective-permute-start.13) | collective-permute-done | bytes 262176 | tf_op jit(solution)/shard_map/ppermute | solution.py:43
  69.3 3.4 %all-to-all-start.1 = ((bf16[8,128,128]{2,1,0:T(8,128)(2,1)}), bf16[8,128,128]{2,1,0:T(8,128)(2,1)S(1)}, u32[]{:S(2)}, u32[]{:S(2)}) async-start(bf16[8,128,128]{2,1,0:T(8,128)(2,1)} %ladder.3), calls=%async_computation.1 | async-start | bytes 524288 | tf_op jit(solution)/shard_map/all_to_all | solution.py:268
  72.7 0.9 %copy-done.4 = bf16[8,128,128]{2,1,0:T(8,128)(2,1)S(1)} copy-done((bf16[8,128,128]{2,1,0:T(8,128)(2,1)S(1)}, bf16[8,128,128]{2,1,0:T(8,128)(2,1)}, u32[]{:S(2)}) %copy-start.4) | copy-done | bytes 262168
  73.7 0.9 %copy-done.10 = bf16[8,128,128]{2,1,0:T(8,128)(2,1)S(1)} copy-done((bf16[8,128,128]{2,1,0:T(8,128)(2,1)S(1)}, bf16[8,128,128]{2,1,0:T(8,128)(2,1)}, u32[]{:S(2)}) %copy-start.10) | copy-done | bytes 262168
  74.6 1.0 %coupling.3.rest_ref = f32[128,128]{1,0:T(8,128)S(1)} custom-call(s32[4]{0:T(128)S(1)} %copy-done.15, bf16[8,128,128]{2,1,0:T(8,128)(2,1)S(1)} %copy-done.4, bf16[8,128,128]{2,1,0:T(8,128)(2,1)S(1)} %copy-done.10, bf16[4,128,128]{2,1,0:T(8,128)(2,1)S(1)} %bitcast.10, f32[128,128]{1,0:T(8,128)S(1)} %bitcast.14), custom_call_target="tpu_custom_call" | custom-call | tf_op jit(solution)/shard_map/coupling/pallas_call | solution.py:197
  75.7 4.4 %all-to-all-done.1.terms_ref = bf16[8,128,128]{2,1,0:T(8,128)(2,1)S(1)} async-done(((bf16[8,128,128]{2,1,0:T(8,128)(2,1)}), bf16[8,128,128]{2,1,0:T(8,128)(2,1)S(1)}, u32[]{:S(2)}, u32[]{:S(2)}) %all-to-all-start.1) | async-done | bytes 262176 | tf_op jit(solution)/shard_map/all_to_all | solution.py:268
  80.1 1.3 %update.3 = f32[128,128]{1,0:T(8,128)} custom-call(s32[2]{0:T(128)S(1)} %dynamic-slice_reduce_fusion.atoms, bf16[8,128,128]{2,1,0:T(8,128)(2,1)S(1)} %all-to-all-done.1.terms_ref, f32[128,128]{1,0:T(8,128)S(1)} %coupling.3.rest_ref, f32[1,128]{1,0:T(1,128)S(1)} %copy-done.13, f32[128,1]{1,0:T(8,128)S(1)} %copy.12.down_ref, f32[1]{0:T(128)S(6)} %copy.29.shift), custom_call_target="tpu_custom_call" | custom-call | tf_op jit(solution)/shard_map/update/pallas_call | solution.py:216
  (71 shorter events, 6.8 us)
Async XLA Ops:
  1.0 10.6 %collective-permute-start = (bf16[1,128,128]{2,1,0:T(8,128)(2,1)}, bf16[1,128,128]{2,1,0:T(8,128)(2,1)S(1)}, u32[]{:S(2)}, u32[]{:S(2)}) collective-permute-start(bf16[1,128,128]{2,1,0:T(8,128)(2,1)} %param.9), channel_id=1, source_target_pairs={{0,4},{1,5},{2,6},{3,7},{4,0},{5,1},{6,2},{7,3},{8,12},{9,13},{10,... | collective-permute-start | bytes 98312 | tf_op jit(solution)/shard_map/ppermute | solution.py:28
  4.2 4.4 %collective-permute-start.1 = (bf16[1,256,128]{2,1,0:T(8,128)(2,1)}, bf16[1,256,128]{2,1,0:T(8,128)(2,1)S(1)}, u32[]{:S(2)}, u32[]{:S(2)}) collective-permute-start(bf16[1,256,128]{2,1,0:T(8,128)(2,1)} %param.10), channel_id=1, source_target_pairs={{0,4},{1,5},{2,6},{3,7},{4,0},{5,1},{6,2},{7,3},{8,12},{9,13},{10,... | collective-permute-start | bytes 196616 | tf_op jit(solution)/shard_map/ppermute | solution.py:28
  8.6 3.9 %collective-permute-start.2 = (bf16[2,256,128]{2,1,0:T(8,128)(2,1)S(1)}, bf16[2,256,128]{2,1,0:T(8,128)(2,1)S(1)}, u32[]{:S(2)}, u32[]{:S(2)}) collective-permute-start(bf16[2,256,128]{2,1,0:T(8,128)(2,1)S(1)} %constant_dynamic-update-slice_fusion.refs_1_), channel_id=1, source_target_pairs={{0,1},{1,0},{2,3},{3,2},{4,5},{5,4},{6,7},{7,6},{8,9},{9,8},{10,11... | collective-permute-start | bytes 393224 | tf_op jit(solution)/shard_map/ppermute | solution.py:28
  9.9 5.5 %collective-permute-start.6 = (bf16[2,256,128]{2,1,0:T(8,128)(2,1)S(1)}, bf16[2,256,128]{2,1,0:T(8,128)(2,1)S(1)}, u32[]{:S(2)}, u32[]{:S(2)}) collective-permute-start(bf16[2,256,128]{2,1,0:T(8,128)(2,1)S(1)} %constant_dynamic-update-slice_fusion.refs_1_), channel_id=1, source_target_pairs={{0,2},{1,3},{2,0},{3,1},{4,6},{5,7},{6,4},{7,5},{8,10},{9,11},{10,... | collective-permute-start | bytes 393224 | tf_op jit(solution)/shard_map/ppermute | solution.py:28
  11.6 5.8 %collective-permute-start.7 = (bf16[2,256,128]{2,1,0:T(8,128)(2,1)S(1)}, bf16[2,256,128]{2,1,0:T(8,128)(2,1)S(1)}, u32[]{:S(2)}, u32[]{:S(2)}) collective-permute-start(bf16[2,256,128]{2,1,0:T(8,128)(2,1)S(1)} %constant_dynamic-update-slice_fusion.refs_1_), channel_id=1, source_target_pairs={{0,3},{1,2},{2,1},{3,0},{4,7},{5,6},{6,5},{7,4},{8,11},{9,10},{10,... | collective-permute-start | bytes 393224 | tf_op jit(solution)/shard_map/ppermute | solution.py:28
  12.5 11.1 %collective-permute-start.3 = (bf16[2,128,128]{2,1,0:T(8,128)(2,1)S(1)}, bf16[2,128,128]{2,1,0:T(8,128)(2,1)S(1)}, u32[]{:S(2)}, u32[]{:S(2)}) collective-permute-start(bf16[2,128,128]{2,1,0:T(8,128)(2,1)S(1)} %pad_maximum_fusion.refs_2_), channel_id=1, source_target_pairs={{0,1},{1,0},{2,3},{3,2},{4,5},{5,4},{6,7},{7,6},{8,9},{9,8},{10,11... | collective-permute-start | bytes 196616 | tf_op jit(solution)/shard_map/ppermute | solution.py:28
  13.7 9.8 %collective-permute-start.4 = (bf16[2,128,128]{2,1,0:T(8,128)(2,1)S(1)}, bf16[2,128,128]{2,1,0:T(8,128)(2,1)S(1)}, u32[]{:S(2)}, u32[]{:S(2)}) collective-permute-start(bf16[2,128,128]{2,1,0:T(8,128)(2,1)S(1)} %pad_maximum_fusion.refs_2_), channel_id=1, source_target_pairs={{0,2},{1,3},{2,0},{3,1},{4,6},{5,7},{6,4},{7,5},{8,10},{9,11},{10,... | collective-permute-start | bytes 196616 | tf_op jit(solution)/shard_map/ppermute | solution.py:28
  15.4 8.1 %collective-permute-start.5 = (bf16[2,128,128]{2,1,0:T(8,128)(2,1)S(1)}, bf16[2,128,128]{2,1,0:T(8,128)(2,1)S(1)}, u32[]{:S(2)}, u32[]{:S(2)}) collective-permute-start(bf16[2,128,128]{2,1,0:T(8,128)(2,1)S(1)} %pad_maximum_fusion.refs_2_), channel_id=1, source_target_pairs={{0,3},{1,2},{2,1},{3,0},{4,7},{5,6},{6,5},{7,4},{8,11},{9,10},{10,... | collective-permute-start | bytes 196616 | tf_op jit(solution)/shard_map/ppermute | solution.py:28
  23.5 16.8 %copy-start.16 = (s32[8,2]{0,1:T(2,128)S(1)}, s32[8,2]{0,1:T(2,128)}, u32[]{:S(2)}) copy-start(s32[8,2]{0,1:T(2,128)} %param.16) | copy-start | bytes 196
  23.5 16.9 %copy-start.13 = (f32[1,128]{1,0:T(1,128)S(1)}, f32[1,128]{1,0:T(1,128)}, u32[]{:S(2)}) copy-start(f32[1,128]{1,0:T(1,128)} %across_ref.3) | copy-start | bytes 1540
  23.5 17.7 %copy-start.17 = (s32[1,4]{1,0:T(1,128)S(1)}, s32[1,4]{1,0:T(1,128)}, u32[]{:S(2)}) copy-start(s32[1,4]{1,0:T(1,128)} %param.17) | copy-start | bytes 52
  23.7 9.2 %copy-start.5 = (bf16[8,128,128]{2,1,0:T(8,128)(2,1)}, bf16[8,128,128]{2,1,0:T(8,128)(2,1)S(1)}, u32[]{:S(2)}) copy-start(bf16[8,128,128]{2,1,0:T(8,128)(2,1)S(1)} %constant_dynamic-update-slice_fusion.2.own_ref) | copy-start | bytes 786436
  23.7 10.9 %collective-permute-start.8 = (bf16[8,128,128]{2,1,0:T(8,128)(2,1)S(1)}, bf16[8,128,128]{2,1,0:T(8,128)(2,1)S(1)}, u32[]{:S(2)}, u32[]{:S(2)}) collective-permute-start(bf16[8,128,128]{2,1,0:T(8,128)(2,1)S(1)} %constant_dynamic-update-slice_fusion.2.own_ref), channel_id=1, source_target_pairs={{8,0},{16,8},{24,16},{9,1},{17,9},{25,17},{10,2},{18,10},{26,18},{... | collective-permute-start | bytes 786440 | tf_op jit(solution)/shard_map/ppermute | solution.py:43
  32.9 0.7 copy-start
  34.6 0.7 copy-start.7
  35.3 13.4 %all-to-all-start = ((bf16[8,128,128]{2,1,0:T(8,128)(2,1)}), bf16[8,128,128]{2,1,0:T(8,128)(2,1)S(1)}, u32[]{:S(2)}, u32[]{:S(2)}) async-start(bf16[8,128,128]{2,1,0:T(8,128)(2,1)} %copy-done), calls=%async_computation | async-start | bytes 524288 | tf_op jit(solution)/shard_map/all_to_all | solution.py:268
  41.8 0.9 %copy-start.1 = (bf16[1,4,128,128]{3,2,1,0:T(8,128)(2,1)S(1)}, bf16[1,4,128,128]{3,2,1,0:T(8,128)(2,1)}, u32[]{:S(2)}) copy-start(bf16[1,4,128,128]{3,2,1,0:T(8,128)(2,1)} %param.12) | copy-start | bytes 393220
  42.7 0.9 %copy-start.6 = (bf16[8,128,128]{2,1,0:T(8,128)(2,1)S(1)}, bf16[8,128,128]{2,1,0:T(8,128)(2,1)}, u32[]{:S(2)}) copy-start(bf16[8,128,128]{2,1,0:T(8,128)(2,1)} %copy-done.5) | copy-start | bytes 786436
  43.6 0.9 %copy-start.8 = (bf16[8,128,128]{2,1,0:T(8,128)(2,1)S(1)}, bf16[8,128,128]{2,1,0:T(8,128)(2,1)}, u32[]{:S(2)}) copy-start(bf16[8,128,128]{2,1,0:T(8,128)(2,1)} %copy-done.7) | copy-start | bytes 786436
  44.6 0.8 %copy-start.11 = (f32[1,128,128]{2,1,0:T(8,128)S(1)}, f32[1,128,128]{2,1,0:T(8,128)}, u32[]{:S(2)}) copy-start(f32[1,128,128]{2,1,0:T(8,128)} %param.13) | copy-start | bytes 196612
  49.3 23.5 %copy-start.2 = (bf16[1,4,128,128]{3,2,1,0:T(8,128)(2,1)S(1)}, bf16[1,4,128,128]{3,2,1,0:T(8,128)(2,1)}, u32[]{:S(2)}) copy-start(bf16[1,4,128,128]{3,2,1,0:T(8,128)(2,1)} %param.12) | copy-start | bytes 393220
  49.3 23.4 %copy-start.12 = (f32[1,128,128]{2,1,0:T(8,128)S(1)}, f32[1,128,128]{2,1,0:T(8,128)}, u32[]{:S(2)}) copy-start(f32[1,128,128]{2,1,0:T(8,128)} %param.13) | copy-start | bytes 196612
  49.3 23.4 %copy-start.15 = (s32[4]{0:T(128)S(1)}, s32[4]{0:T(128)}, u32[]{:S(2)}) copy-start(s32[4]{0:T(128)} %copy-done.14) | copy-start | bytes 52
  49.3 4.9 %collective-permute-start.9 = (bf16[1,128,128]{2,1,0:T(8,128)(2,1)S(1)}, bf16[1,128,128]{2,1,0:T(8,128)(2,1)S(1)}, u32[]{:S(2)}, u32[]{:S(2)}) collective-permute-start(bf16[1,128,128]{2,1,0:T(8,128)(2,1)S(1)} %bitcast.11), channel_id=1, source_target_pairs={{0,4},{1,5},{2,6},{3,7},{4,0},{5,1},{6,2},{7,3},{8,12},{9,13},{10,... | collective-permute-start | bytes 98312 | tf_op jit(solution)/shard_map/ppermute | solution.py:28
  54.2 3.2 %collective-permute-start.10 = (bf16[2,128,128]{2,1,0:T(8,128)(2,1)S(1)}, bf16[2,128,128]{2,1,0:T(8,128)(2,1)S(1)}, u32[]{:S(2)}, u32[]{:S(2)}) collective-permute-start(bf16[2,128,128]{2,1,0:T(8,128)(2,1)S(1)} %pad_maximum_fusion.1.refs_2_), channel_id=1, source_target_pairs={{0,1},{1,0},{2,3},{3,2},{4,5},{5,4},{6,7},{7,6},{8,9},{9,8},{10,11... | collective-permute-start | bytes 196616 | tf_op jit(solution)/shard_map/ppermute | solution.py:28
  54.4 3.4 %collective-permute-start.11 = (bf16[2,128,128]{2,1,0:T(8,128)(2,1)S(1)}, bf16[2,128,128]{2,1,0:T(8,128)(2,1)S(1)}, u32[]{:S(2)}, u32[]{:S(2)}) collective-permute-start(bf16[2,128,128]{2,1,0:T(8,128)(2,1)S(1)} %pad_maximum_fusion.1.refs_2_), channel_id=1, source_target_pairs={{0,2},{1,3},{2,0},{3,1},{4,6},{5,7},{6,4},{7,5},{8,10},{9,11},{10,... | collective-permute-start | bytes 196616 | tf_op jit(solution)/shard_map/ppermute | solution.py:28
  54.4 5.1 %collective-permute-start.12 = (bf16[2,128,128]{2,1,0:T(8,128)(2,1)S(1)}, bf16[2,128,128]{2,1,0:T(8,128)(2,1)S(1)}, u32[]{:S(2)}, u32[]{:S(2)}) collective-permute-start(bf16[2,128,128]{2,1,0:T(8,128)(2,1)S(1)} %pad_maximum_fusion.1.refs_2_), channel_id=1, source_target_pairs={{0,3},{1,2},{2,1},{3,0},{4,7},{5,6},{6,5},{7,4},{8,11},{9,10},{10,... | collective-permute-start | bytes 196616 | tf_op jit(solution)/shard_map/ppermute | solution.py:28
  59.6 7.2 %copy-start.3 = (bf16[8,128,128]{2,1,0:T(8,128)(2,1)}, bf16[8,128,128]{2,1,0:T(8,128)(2,1)S(1)}, u32[]{:S(2)}) copy-start(bf16[8,128,128]{2,1,0:T(8,128)(2,1)S(1)} %constant_dynamic-update-slice_fusion.10.own_ref) | copy-start | bytes 786436
  59.6 9.0 %collective-permute-start.13 = (bf16[8,128,128]{2,1,0:T(8,128)(2,1)S(1)}, bf16[8,128,128]{2,1,0:T(8,128)(2,1)S(1)}, u32[]{:S(2)}, u32[]{:S(2)}) collective-permute-start(bf16[8,128,128]{2,1,0:T(8,128)(2,1)S(1)} %constant_dynamic-update-slice_fusion.10.own_ref), channel_id=1, source_target_pairs={{8,0},{16,8},{24,16},{9,1},{17,9},{25,17},{10,2},{18,10},{26,18},{... | collective-permute-start | bytes 786440 | tf_op jit(solution)/shard_map/ppermute | solution.py:43
  69.3 10.8 %all-to-all-start.1 = ((bf16[8,128,128]{2,1,0:T(8,128)(2,1)}), bf16[8,128,128]{2,1,0:T(8,128)(2,1)S(1)}, u32[]{:S(2)}, u32[]{:S(2)}) async-start(bf16[8,128,128]{2,1,0:T(8,128)(2,1)} %ladder.3), calls=%async_computation.1 | async-start | bytes 524288 | tf_op jit(solution)/shard_map/all_to_all | solution.py:268
  72.7 1.0 %copy-start.4 = (bf16[8,128,128]{2,1,0:T(8,128)(2,1)S(1)}, bf16[8,128,128]{2,1,0:T(8,128)(2,1)}, u32[]{:S(2)}) copy-start(bf16[8,128,128]{2,1,0:T(8,128)(2,1)} %copy-done.3) | copy-start | bytes 786436
  73.7 0.9 %copy-start.10 = (bf16[8,128,128]{2,1,0:T(8,128)(2,1)S(1)}, bf16[8,128,128]{2,1,0:T(8,128)(2,1)}, u32[]{:S(2)}) copy-start(bf16[8,128,128]{2,1,0:T(8,128)(2,1)} %copy-done.9) | copy-start | bytes 786436
  (2 other events, 1.2 us)

commit v2 on v1

--- a/solution.py
+++ b/solution.py
@@ -9,6 +9,7 @@
 ITERS = 2
 F32 = jnp.float32
 BF16 = jnp.bfloat16
+CONTRACT_LAST = (((1,), (1,)), ((), ()))
 
 
 def vmem_spec():
@@ -38,9 +39,17 @@
     return [pair] + [exchange(pair, axis, j) for j in range(1, half)]
 
 
+def stack_offsets(found):
+    return jnp.concatenate([g[r : r + 1] for r in range(2) for g in found], axis=0)
+
+
 def from_next(value, axis):
     count = lax.axis_size(axis)
     return lax.ppermute(value, axis, [(d, d - 1) for d in range(1, count)])
+
+
+def all_to_all(value):
+    return lax.all_to_all(value, "dev", split_axis=0, concat_axis=0, tiled=True)
 
 
 def project_kernel(given, slots, *refs):
@@ -100,8 +109,12 @@
     )(slots, *group_bases, factor_block)
 
 
-def ladder_kernel(given, slots, pairs, *refs):
-    amp_refs, (proj_ref, out_ref, twice, mixed, narrow, sems) = refs[:given], refs[given:]
+def ladder_kernel(given, spread, chunked, slots, pairs, devices, *refs):
+    amp_refs, (proj_ref, out_ref, amp_rows, twice, mixed), tail = (
+        refs[:given],
+        refs[given : given + 5],
+        refs[given + 5 :],
+    )
     half, npno = proj_ref.shape[1], proj_ref.shape[2]
     s = pl.program_id(0)
 
@@ -109,14 +122,22 @@
     def _():
         twice[...] = jnp.zeros_like(twice)
 
-    for j in range(given):
-
-        @pl.when(lax.rem(slots[s], given) == j)
-        def _():
-            amp = amp_refs[j][slots[s] // given]
-            twice[pl.ds(0, npno), pl.ds(0, npno)] = amp
-            twice[pl.ds(npno, npno), pl.ds(npno, npno)] = amp
-
+    if chunked:
+        pair = jnp.maximum(pairs[s], 0)
+        rows = amp_refs[0].shape[2]
+        for o in range(2 * given):
+            first = pl.multiple_of(devices[o] * rows, rows)
+            amp_rows[pl.ds(first, rows), :] = amp_refs[o % given][o // given, pair]
+    else:
+        for j in range(given):
+
+            @pl.when(lax.rem(slots[s], given) == j)
+            def _():
+                amp_rows[...] = amp_refs[j][slots[s] // given]
+
+    amp = amp_rows[...]
+    twice[pl.ds(0, npno), pl.ds(0, npno)] = amp
+    twice[pl.ds(npno, npno), pl.ds(npno, npno)] = amp
     flat = proj_ref[0].reshape(half * npno, 2 * npno)
     mixed[...] = jnp.dot(flat, twice[...], preferred_element_type=F32).astype(BF16)
     total = jnp.zeros((npno, npno), F32)
@@ -124,9 +145,13 @@
         total = total + lax.dot_general(
             mixed[pl.ds(m * npno, npno), :],
             proj_ref[0, m],
-            (((1,), (1,)), ((), ())),
+            CONTRACT_LAST,
             preferred_element_type=F32,
         )
+    if not spread:
+        out_ref[0] = total.astype(BF16)
+        return
+    narrow, sems = tail
     narrow[s] = total.astype(BF16)
 
     def copy(t):
@@ -145,28 +170,34 @@
                 copy(t).wait()
 
 
-def ladder(count, slots, pairs, group_amps, projected):
+def ladder(spread, slots, pairs, devices, group_amps, projected):
+    count = devices.shape[0]
     given = len(group_amps)
-    npno = group_amps[0].shape[1]
-    half = projected.shape[1]
+    chunked = group_amps[0].ndim == 4
+    half, npno = projected.shape[1:3]
 
     def kernel(*refs):
-        ladder_kernel(given, *refs)
-
+        ladder_kernel(given, spread, chunked, *refs)
+
+    whole = group_amps[0].shape
+    scratch = [
+        pltpu.VMEM((npno, npno), BF16),
+        pltpu.VMEM((2 * npno, 2 * npno), BF16),
+        pltpu.VMEM((half * npno, 2 * npno), BF16),
+    ]
+    if spread:
+        scratch += [pltpu.VMEM((CAP, npno, npno), BF16), pltpu.SemaphoreType.DMA((CAP,))]
     return pl.pallas_call(
         kernel,
         grid=(CAP,),
-        in_specs=[smem_spec()] * 2
-        + [pl.BlockSpec(group_amps[0].shape, lambda s: (0, 0, 0))] * given
+        in_specs=[smem_spec()] * 3
+        + [pl.BlockSpec(whole, lambda s: (0,) * len(whole))] * given
         + [pl.BlockSpec((1, half, npno, 2 * npno), lambda s: (s, 0, 0, 0))],
-        out_specs=pl.BlockSpec(memory_space=pl.ANY),
-        out_shape=jax.ShapeDtypeStruct((count, npno, npno), BF16),
-        scratch_shapes=[
-            pltpu.VMEM((2 * npno, 2 * npno), BF16),
-            pltpu.VMEM((half * npno, 2 * npno), BF16),
-            pltpu.VMEM((CAP, npno, npno), BF16),
-            pltpu.SemaphoreType.DMA((CAP,)),
-        ],
+        out_specs=pl.BlockSpec(memory_space=pltpu.HBM)
+        if spread
+        else pl.BlockSpec((1, npno, npno), lambda s: (s, 0, 0)),
+        out_shape=jax.ShapeDtypeStruct((count if spread else CAP, npno, npno), BF16),
+        scratch_shapes=scratch,
         compiler_params=params(24),
         cost_estimate=pl.CostEstimate(
             flops=0,
@@ -174,34 +205,93 @@
             transcendentals=0,
         ),
         name="ladder",
-    )(slots, pairs, *group_amps, projected)
-
-
-def coupling_kernel(near, own_ref, next_ref, inter_ref, ints_ref, out_ref):
+    )(slots, pairs, devices, *group_amps, projected)
+
+
+def coupled(near, devices, own_ref, next_ref, inter_ref, total, amp_rows):
     count = own_ref.shape[0]
-    total = ints_ref[...]
     for n in range(inter_ref.shape[0]):
         at = near[n]
-        own = own_ref[jnp.minimum(at, count - 1)]
-        far = next_ref[jnp.maximum(at - count, 0)]
-        amp = jnp.where(at < count, own, far)
+        low, high = jnp.minimum(at, count - 1), jnp.maximum(at - count, 0)
+        if len(own_ref.shape) == 4:
+            rows = own_ref.shape[2]
+            for o in range(count):
+                first = pl.multiple_of(devices[o] * rows, rows)
+                amp_rows[pl.ds(first, rows), :] = jnp.where(
+                    at < count, own_ref[o, low], next_ref[o, high]
+                )
+            amp = amp_rows[...]
+        else:
+            amp = jnp.where(
+                at < count, own_ref[low ^ devices[0]], next_ref[high ^ devices[0]]
+            )
         inter = inter_ref[n]
         mixed = jnp.dot(inter, amp, preferred_element_type=F32).astype(BF16)
         total = total + lax.dot_general(
-            mixed, inter, (((1,), (1,)), ((), ())), preferred_element_type=F32
+            mixed, inter, CONTRACT_LAST, preferred_element_type=F32
         )
-    out_ref[...] = total
-
-
-def coupling(near, own, following, inter, ints):
+    return total
+
+
+def coupling_kernel(near, devices, own_ref, next_ref, inter_ref, ints_ref, out_ref, amp_rows):
+    out_ref[...] = coupled(near, devices, own_ref, next_ref, inter_ref, ints_ref[...], amp_rows)
+
+
+def coupling(near, devices, own, following, inter, ints):
     return pl.pallas_call(
         coupling_kernel,
-        in_specs=[smem_spec()] + [vmem_spec()] * 4,
+        in_specs=[smem_spec()] * 2 + [vmem_spec()] * 4,
         out_specs=vmem_spec(),
         out_shape=jax.ShapeDtypeStruct(ints.shape, F32),
+        scratch_shapes=[pltpu.VMEM(ints.shape, BF16)],
         compiler_params=params(16),
         name="coupling",
-    )(near, own, following, inter, ints)
+    )(near, devices, own, following, inter, ints)
+
+
+def scatter_kernel(
+    near, devices, own_ref, next_ref, inter_ref, ints_ref, across, down, shift, terms_ref, out_ref, amp_rows
+):
+    rest = coupled(near, devices, own_ref, next_ref, inter_ref, ints_ref[...], amp_rows)
+    scale = -1.0 / (down[...] + across[...] + shift[0])
+    count, _, rows, npno = out_ref.shape
+    parts = [terms_ref[s] for s in range(CAP)] + [(rest * scale).astype(BF16), scale.astype(BF16)]
+    for t, part in enumerate(parts):
+        out_ref[:, t] = part.reshape(count, rows, npno)
+
+
+def scatter_rows(near, devices, own, following, inter, ints, across, down, shift, terms):
+    count, npno = own.shape[0], ints.shape[1]
+    return pl.pallas_call(
+        scatter_kernel,
+        in_specs=[smem_spec()] * 2 + [vmem_spec()] * 6 + [smem_spec(), vmem_spec()],
+        out_specs=vmem_spec(),
+        out_shape=jax.ShapeDtypeStruct((count, CAP + 2, npno // count, npno), BF16),
+        scratch_shapes=[pltpu.VMEM(ints.shape, BF16)],
+        compiler_params=params(16),
+        name="scatter_rows",
+    )(near, devices, own, following, inter, ints, across, down, shift, terms)
+
+
+def update_rows_kernel(atoms, ranks, rows_ref, out_ref):
+    for p in range(out_ref.shape[0]):
+        total = jnp.zeros(out_ref.shape[1:], F32)
+        for t in range(atoms.shape[1]):
+            total = total + rows_ref[atoms[p, t], ranks[p, t]].astype(F32)
+        scale = rows_ref[p, CAP + 1].astype(F32)
+        out_ref[p] = (total * scale + rows_ref[p, CAP].astype(F32)).astype(BF16)
+
+
+def update_rows(atoms, ranks, arrived):
+    count, _, rows, npno = arrived.shape
+    return pl.pallas_call(
+        update_rows_kernel,
+        in_specs=[smem_spec()] * 2 + [vmem_spec()],
+        out_specs=vmem_spec(),
+        out_shape=jax.ShapeDtypeStruct((count, rows, npno), BF16),
+        compiler_params=params(16),
+        name="update_rows",
+    )(atoms, ranks, arrived)
 
 
 def update_kernel(atoms, terms_ref, rest_ref, across_ref, down_ref, shift, out_ref):
@@ -237,40 +327,47 @@
     me = lax.axis_index("dev")
     count = lax.axis_size("dev")
     places = jnp.arange(count, dtype=jnp.int32)
+    devices = places ^ me
     listed = jnp.any(pair_atoms == me, axis=1)
-    rank = jnp.sum((places[None, :] < places[:, None]) & listed[None, :], axis=1)
+    before = places[None, :] < places[:, None]
+    rank = jnp.sum(before & listed[None, :], axis=1)
     chosen = listed[None, :] & (rank[None, :] == jnp.arange(CAP)[:, None])
     pairs = jnp.sum(jnp.where(chosen, places[None, :] + 1, 0), axis=1) - 1
     slots = jnp.where(pairs >= 0, pairs ^ me, 0)
+    same = jnp.any(pair_atoms[:, :, None, None] == pair_atoms[None, None, :, :], axis=3)
+    ranks = jnp.sum((before[:, None, :] & same).astype(jnp.int32), axis=2)
     atoms = pair_atoms[me]
     near = pair_next[0]
-    near = jnp.where(near < count, near ^ me, ((near - count) ^ me) + count)
     across = pno_energies
     down = pno_energies.reshape(-1, 1)
     inter = intersections[0]
     ints = pair_integrals[0]
+    chunked = ints.shape[0] % (16 * count) == 0
 
     group_bases = gather_near(gather_across(bases, "dev"), "dev")
-    first, slots, pairs = lax.optimization_barrier((amplitudes, slots, pairs))
     pair_amps, group_bases[1] = lax.optimization_barrier(
-        (gather_across(first, "dev"), group_bases[1])
+        (gather_across(amplitudes, "dev"), group_bases[1])
     )
     group_amps = gather_near(pair_amps, "dev")
     projected = project(slots, group_bases, factors[0])
     group_amps, projected = lax.optimization_barrier((group_amps, projected))
     for iteration in range(ITERS):
-        stacked = jnp.concatenate(
-            [g[r : r + 1] for r in range(2) for g in group_amps], axis=0
-        )
+        last = iteration + 1 == ITERS
+        stacked = stack_offsets(group_amps)
         following = from_next(stacked, "grp")
-        terms = ladder(count, slots, pairs, group_amps, projected)
-        terms, following = lax.optimization_barrier((terms, following))
-        arrived = lax.all_to_all(terms, "dev", split_axis=0, concat_axis=0, tiled=True)
-        rest = coupling(near, stacked, following, inter, ints)
-        last = iteration + 1 == ITERS
-        update = update_pair(
-            atoms, arrived, rest, across, down, pair_shift, F32 if last else BF16
-        )
+        direct = last or not chunked
+        terms = ladder(direct, slots, pairs, devices, group_amps, projected)
+        if direct:
+            arrived = all_to_all(terms)
+            rest = coupling(near, devices, stacked, following, inter, ints)
+            update = update_pair(
+                atoms, arrived, rest, across, down, pair_shift, F32 if last else BF16
+            )
+        else:
+            rows = scatter_rows(
+                near, devices, stacked, following, inter, ints, across, down, pair_shift, terms
+            )
+            update = update_rows(pair_atoms, ranks, all_to_all(rows))
         if not last:
             group_amps = gather_near(gather_across(update[None], "dev"), "dev")
     return update[None]

time: 82.1 us -> 94.3 us (1.15)
  local copies, waits for them, and re-layouts: 9.5 us -> 19.3 us
  starting transfers between devices: 30.5 us -> 34.2 us
  waiting for transfers between devices: 21.8 us -> 18.4 us
  Pallas kernels: 16.8 us -> 17.9 us
  other arithmetic: 1.73 us -> 2.7 us
    unnamed x51 -> x46, local copies, waits for them, and re-layouts: 9.17 us -> 17 us
    ppermute x12, waiting for transfers between devices: 12.4 us -> 6.63 us  [exchange(): return lax.ppermute(value, axis, [(d, d ^ offset) for d in range(count)])]
    ppermute x2, waiting for transfers between devices: 2.83 us -> 5.17 us  [from_next(): return lax.ppermute(value, axis, [(d, d - 1) for d in range(1, count)])]
    ppermute x12, starting transfers between devices: 12.6 us -> 14.8 us  [exchange(): return lax.ppermute(value, axis, [(d, d ^ offset) for d in range(count)])]
    pallas_call x4 -> x5, Pallas kernels: 8.85 us -> 10.5 us  [the longest x2 6.61 us: ladder(): pl.pallas_call(kernel, grid=(CAP,), in_specs=[smem_spec()] * 3 + [pl.Bloc...]
    all_to_all x2, starting transfers between devices: 8.41 us -> 9.78 us  [all_to_all(): return lax.all_to_all(value, 'dev', split_axis=0, concat_axis=0, tiled=True)]
    concatenate x2, local copies, waits for them, and re-layouts: 0.02 us -> 1.22 us  [stack_offsets(): jnp.concatenate([g[r:r + 1] for r in range(2) for g in found], axis=0)]
    pallas_call x2 -> x1, Pallas kernels: 1.89 us -> 1.26 us  [update_pair(): pl.pallas_call(update_kernel, in_specs=[smem_spec()] + [vmem_spec()] * 4...]
  transfers between devices with their start and end apart: 16 -> 16, of which waited for: 11 -> 5; matrix products, arithmetic and copies ran while one was open for 2% -> 12% of each run, Pallas kernels for 18% -> 11%
where the time goes in v2:
time: 94.3 us; the launch traced here: 93.4 us
  starting transfers between devices  34.2 us (36%)
  local copies, waits for them, and re-layouts  19.3 us (20%)
  waiting for transfers between devices  18.4 us (20%)
  Pallas kernels  17.9 us (19%)
  other arithmetic  2.7 us (3%)
    unnamed x46, local copies, waits for them, and re-layouts  17 us
    ppermute x12, starting transfers between devices, exchange(): return lax.ppermute(value, axis, [(d, d ^ offset) for d in range(count)])  14.8 us
    all_to_all x2, starting transfers between devices, all_to_all(): return lax.all_to_all(value, 'dev', split_axis=0, concat_axis=0, tiled=True)  9.78 us
    ppermute x2, starting transfers between devices, from_next(): return lax.ppermute(value, axis, [(d, d - 1) for d in range(1, count)])  9.53 us
    ppermute x12, waiting for transfers between devices, exchange(): return lax.ppermute(value, axis, [(d, d ^ offset) for d in range(count)])  6.63 us
    all_to_all x2, waiting for transfers between devices, all_to_all(): return lax.all_to_all(value, 'dev', split_axis=0, concat_axis=0, tiled=True)  6.61 us
    pallas_call x2, Pallas kernels, ladder(): pl.pallas_call(kernel, grid=(CAP,), in_specs=[smem_spec()] * 3 + [pl.Bloc...  6.61 us
    pallas_call x1, Pallas kernels, project(): pl.pallas_call(kernel, grid=(aux // step,), in_specs=[smem_spec()] + [pl....  6.11 us
  transfers between devices with their start and end apart: 16, of which 5 were waited for; matrix products, arithmetic and copies ran while one was open for 12% of the time, Pallas kernels for 11%

profile of v2, /device:TPU:1, one launch (start us, length us, event | category | flops | bytes accessed | tf_op | source)
XLA Modules:
  0.0 93.4 jit_solution(13098149061012141094)
XLA Ops:
  0.0 3.1 %collective-permute-start.1 = (bf16[1,256,128]{2,1,0:T(8,128)(2,1)}, bf16[1,256,128]{2,1,0:T(8,128)(2,1)S(1)}, u32[]{:S(2)}, u32[]{:S(2)}) collective-permute-start(bf16[1,256,128]{2,1,0:T(8,128)(2,1)} %param.10), channel_id=1, source_target_pairs={{0,4},{1,5},{2,6},{3,7},{4,0},{5,1},{6,2},{7,3},{8,12},{9,13},{10,... | collective-permute-start | bytes 196616 | tf_op jit(solution)/shard_map/ppermute | solution.py:29
  3.2 0.9 constant_dynamic-update-slice_fusion.1
  5.0 1.4 %collective-permute-start.2 = (bf16[2,256,128]{2,1,0:T(8,128)(2,1)S(1)}, bf16[2,256,128]{2,1,0:T(8,128)(2,1)S(1)}, u32[]{:S(2)}, u32[]{:S(2)}) collective-permute-start(bf16[2,256,128]{2,1,0:T(8,128)(2,1)S(1)} %constant_dynamic-update-slice_fusion.refs_1_), channel_id=1, source_target_pairs={{0,1},{1,0},{2,3},{3,2},{4,5},{5,4},{6,7},{7,6},{8,9},{9,8},{10,11... | collective-permute-start | bytes 393224 | tf_op jit(solution)/shard_map/ppermute | solution.py:29
  6.4 3.5 %collective-permute-start.6 = (bf16[2,256,128]{2,1,0:T(8,128)(2,1)S(1)}, bf16[2,256,128]{2,1,0:T(8,128)(2,1)S(1)}, u32[]{:S(2)}, u32[]{:S(2)}) collective-permute-start(bf16[2,256,128]{2,1,0:T(8,128)(2,1)S(1)} %constant_dynamic-update-slice_fusion.refs_1_), channel_id=1, source_target_pairs={{0,2},{1,3},{2,0},{3,1},{4,6},{5,7},{6,4},{7,5},{8,10},{9,11},{10,... | collective-permute-start | bytes 393224 | tf_op jit(solution)/shard_map/ppermute | solution.py:29
  9.9 0.8 pad_maximum_fusion.refs_3_
  10.7 1.2 %collective-permute-start.3 = (bf16[2,128,128]{2,1,0:T(8,128)(2,1)S(1)}, bf16[2,128,128]{2,1,0:T(8,128)(2,1)S(1)}, u32[]{:S(2)}, u32[]{:S(2)}) collective-permute-start(bf16[2,128,128]{2,1,0:T(8,128)(2,1)S(1)} %pad_maximum_fusion.refs_3_), channel_id=1, source_target_pairs={{0,1},{1,0},{2,3},{3,2},{4,5},{5,4},{6,7},{7,6},{8,9},{9,8},{10,11... | collective-permute-start | bytes 196616 | tf_op jit(solution)/shard_map/ppermute | solution.py:29
  11.9 2.4 %collective-permute-start.4 = (bf16[2,128,128]{2,1,0:T(8,128)(2,1)S(1)}, bf16[2,128,128]{2,1,0:T(8,128)(2,1)S(1)}, u32[]{:S(2)}, u32[]{:S(2)}) collective-permute-start(bf16[2,128,128]{2,1,0:T(8,128)(2,1)S(1)} %pad_maximum_fusion.refs_3_), channel_id=1, source_target_pairs={{0,2},{1,3},{2,0},{3,1},{4,6},{5,7},{6,4},{7,5},{8,10},{9,11},{10,... | collective-permute-start | bytes 196616 | tf_op jit(solution)/shard_map/ppermute | solution.py:29
  14.3 1.5 %collective-permute-done.7.refs_4_ = bf16[2,256,128]{2,1,0:T(8,128)(2,1)S(1)} collective-permute-done((bf16[2,256,128]{2,1,0:T(8,128)(2,1)S(1)}, bf16[2,256,128]{2,1,0:T(8,128)(2,1)S(1)}, u32[]{:S(2)}, u32[]{:S(2)}) %collective-permute-start.7) | collective-permute-done | bytes 131104 | tf_op jit(solution)/shard_map/ppermute | solution.py:29
  15.9 6.1 %project.1.refs_7_ = bf16[3,16,128,256]{3,2,1,0:T(8,128)(2,1)S(1)} custom-call(s32[3]{0:T(128)S(1)} %get-tuple-element.20.refs_0_, bf16[2,256,128]{2,1,0:T(8,128)(2,1)S(1)} %constant_dynamic-update-slice_fusion.refs_1_, bf16[2,256,128]{2,1,0:T(8,128)(2,1)S(1)} %collective-permute-done.2.refs_2_, bf16[2,256,128]{2,1,0:T(8,128)(2,1)S(1)} %collective-permute-done.6.refs_3_, ...), custom_call_target="tpu_custom_call" | custom-call | flops 2415919104 | bytes 4194304 | tf_op jit(solution)/shard_map/project/pallas_call | solution.py:89
  27.0 4.3 %collective-permute-start.8 = (bf16[8,128,128]{2,1,0:T(8,128)(2,1)}, bf16[8,128,128]{2,1,0:T(8,128)(2,1)}, u32[]{:S(2)}, u32[]{:S(2)}) collective-permute-start(bf16[8,128,128]{2,1,0:T(8,128)(2,1)} %constant_dynamic-update-slice_fusion.2.own_ref), channel_id=1, source_target_pairs={{8,0},{16,8},{24,16},{9,1},{17,9},{25,17},{10,2},{18,10},{26,18},{... | collective-permute-start | bytes 786440 | tf_op jit(solution)/shard_map/ppermute | solution.py:48
  31.3 0.8 copy.16.atoms
  32.8 0.8 copy-done.5
  33.7 0.8 copy-done.7
  35.1 3.3 %ladder.2.terms_ref = bf16[3,128,128]{2,1,0:T(8,128)(2,1)S(1)} custom-call(s32[3]{0:T(128)S(1)} %copy-done.10, s32[3]{0:T(128)S(1)} %get-tuple-element.19.refs_1_, s32[8]{0:T(128)S(1)} %iota_xor_fusion.refs_2_.devices, bf16[2,128,128]{2,1,0:T(8,128)(2,1)S(1)} %pad_maximum_fusion.refs_3_, bf16[2,128,128]{2,1,0:T(8,128)(2,1)S(1)} %collective-permute-done.3.refs_4_, ...), custom_call_target="tpu_custom_call" | custom-call | bytes 12582912 | tf_op jit(solution)/shard_map/ladder/pallas_call | solution.py:190
  39.2 2.2 %scatter_rows.1 = bf16[8,5,16,128]{3,2,1,0:T(8,128)(2,1)} custom-call(s32[4]{0:T(128)S(1)} %bitcast.15, s32[8]{0:T(128)S(1)} %iota_xor_fusion.refs_2_.devices, bf16[8,128,128]{2,1,0:T(8,128)(2,1)} %constant_dynamic-update-slice_fusion.2.own_ref, bf16[8,128,128]{2,1,0:T(8,128)(2,1)} %collective-permute-done.8.next_ref, bf16[4,128,128]{2,1,0:T(8,128)(2,1)S(1)} %bitcast.8, ...), custom_call_target="tpu_custom_call" | custom-call | tf_op jit(solution)/shard_map/scatter_rows/pallas_call | solution.py:265
  41.3 6.4 %all-to-all-start = ((bf16[8,5,16,128]{3,2,1,0:T(8,128)(2,1)}), bf16[8,5,16,128]{3,2,1,0:T(8,128)(2,1)S(1)}, u32[]{:S(2)}, u32[]{:S(2)}) async-start(bf16[8,5,16,128]{3,2,1,0:T(8,128)(2,1)} %scatter_rows.1), calls=%async_computation | async-start | bytes 327680 | tf_op jit(solution)/shard_map/all_to_all | solution.py:52
  47.7 0.8 compare_reduce_fusion
  48.8 6.6 %all-to-all-done.rows_ref = bf16[8,5,16,128]{3,2,1,0:T(8,128)(2,1)S(1)} async-done(((bf16[8,5,16,128]{3,2,1,0:T(8,128)(2,1)}), bf16[8,5,16,128]{3,2,1,0:T(8,128)(2,1)S(1)}, u32[]{:S(2)}, u32[]{:S(2)}) %all-to-all-start) | async-done | bytes 163872 | tf_op jit(solution)/shard_map/all_to_all | solution.py:52
  56.5 3.3 %collective-permute-done.9 = bf16[1,8,16,128]{3,2,1,0:T(8,128)(2,1)S(1)} collective-permute-done((bf16[1,8,16,128]{3,2,1,0:T(8,128)(2,1)S(1)}, bf16[1,8,16,128]{3,2,1,0:T(8,128)(2,1)S(1)}, u32[]{:S(2)}, u32[]{:S(2)}) %collective-permute-start.9) | collective-permute-done | bytes 32800 | tf_op jit(solution)/shard_map/ppermute | solution.py:29
  59.9 1.0 %collective-permute-start.11 = (bf16[2,8,16,128]{3,2,1,0:T(8,128)(2,1)S(1)}, bf16[2,8,16,128]{3,2,1,0:T(8,128)(2,1)S(1)}, u32[]{:S(2)}, u32[]{:S(2)}) collective-permute-start(bf16[2,8,16,128]{3,2,1,0:T(8,128)(2,1)S(1)} %pad_maximum_fusion.1.refs_3_), channel_id=1, source_target_pairs={{0,2},{1,3},{2,0},{3,1},{4,6},{5,7},{6,4},{7,5},{8,10},{9,11},{10,... | collective-permute-start | bytes 196616 | tf_op jit(solution)/shard_map/ppermute | solution.py:29
  60.9 1.6 %collective-permute-start.12 = (bf16[2,8,16,128]{3,2,1,0:T(8,128)(2,1)S(1)}, bf16[2,8,16,128]{3,2,1,0:T(8,128)(2,1)S(1)}, u32[]{:S(2)}, u32[]{:S(2)}) collective-permute-start(bf16[2,8,16,128]{3,2,1,0:T(8,128)(2,1)S(1)} %pad_maximum_fusion.1.refs_3_), channel_id=1, source_target_pairs={{0,3},{1,2},{2,1},{3,0},{4,7},{5,6},{6,5},{7,4},{8,11},{9,10},{10,... | collective-permute-start | bytes 196616 | tf_op jit(solution)/shard_map/ppermute | solution.py:29
  63.2 1.8 %collective-permute-done.12.refs_6_ = bf16[2,8,16,128]{3,2,1,0:T(8,128)(2,1)S(1)} collective-permute-done((bf16[2,8,16,128]{3,2,1,0:T(8,128)(2,1)S(1)}, bf16[2,8,16,128]{3,2,1,0:T(8,128)(2,1)S(1)}, u32[]{:S(2)}, u32[]{:S(2)}) %collective-permute-start.12) | collective-permute-done | bytes 65568 | tf_op jit(solution)/shard_map/ppermute | solution.py:29
  65.6 3.3 %ladder.3 = bf16[8,128,128]{2,1,0:T(8,128)(2,1)} custom-call(s32[3]{0:T(128)S(1)} %copy-done.11, s32[3]{0:T(128)S(1)} %get-tuple-element.19.refs_1_, s32[8]{0:T(128)S(1)} %iota_xor_fusion.refs_2_.devices, bf16[2,8,16,128]{3,2,1,0:T(8,128)(2,1)S(1)} %pad_maximum_fusion.1.refs_3_, bf16[2,8,16,128]{3,2,1,0:T(8,128)(2,1)S(1)} %collective-permute-done.10.refs_4_, ...), custom_call_target="tpu_custom_call" | custom-call | bytes 12582912 | tf_op jit(solution)/shard_map/ladder/pallas_call | solution.py:190
  68.9 3.4 %all-to-all-start.1 = ((bf16[8,128,128]{2,1,0:T(8,128)(2,1)}), bf16[8,128,128]{2,1,0:T(8,128)(2,1)S(1)}, u32[]{:S(2)}, u32[]{:S(2)}) async-start(bf16[8,128,128]{2,1,0:T(8,128)(2,1)} %ladder.3), calls=%async_computation.1 | async-start | bytes 524288 | tf_op jit(solution)/shard_map/all_to_all | solution.py:52
  74.2 1.4 %constant_dynamic-update-slice_fusion.13 = bf16[8,8,16,128]{3,2,1,0:T(8,128)(2,1)} fusion(bf16[8,8,16,128]{3,2,1,0:T(8,128)(2,1)} %constant_dynamic-update-slice_fusion.14, bf16[1,8,16,128]{3,2,1,0:T(8,128)(2,1)} %copy-done.14), kind=kLoop, calls=%fused_computation.15 | loop fusion | bytes 65536
  77.4 5.2 %collective-permute-start.13 = (bf16[8,8,16,128]{3,2,1,0:T(8,128)(2,1)}, bf16[8,8,16,128]{3,2,1,0:T(8,128)(2,1)S(1)}, u32[]{:S(2)}, u32[]{:S(2)}) collective-permute-start(bf16[8,8,16,128]{3,2,1,0:T(8,128)(2,1)} %constant_dynamic-update-slice_fusion.10.own_ref), channel_id=1, source_target_pairs={{8,0},{16,8},{24,16},{9,1},{17,9},{25,17},{10,2},{18,10},{26,18},{... | collective-permute-start | bytes 786440 | tf_op jit(solution)/shard_map/ppermute | solution.py:48
  82.6 0.9 dynamic-slice_reduce_fusion.atoms
  83.5 5.2 %collective-permute-done.13.next_ref = bf16[8,8,16,128]{3,2,1,0:T(8,128)(2,1)S(1)} collective-permute-done((bf16[8,8,16,128]{3,2,1,0:T(8,128)(2,1)}, bf16[8,8,16,128]{3,2,1,0:T(8,128)(2,1)S(1)}, u32[]{:S(2)}, u32[]{:S(2)}) %collective-permute-start.13) | collective-permute-done | bytes 262176 | tf_op jit(solution)/shard_map/ppermute | solution.py:48
  88.6 0.9 %copy-done.1 = bf16[8,8,16,128]{3,2,1,0:T(8,128)(2,1)S(1)} copy-done((bf16[8,8,16,128]{3,2,1,0:T(8,128)(2,1)S(1)}, bf16[8,8,16,128]{3,2,1,0:T(8,128)(2,1)}, u32[]{:S(2)}) %copy-start.1) | copy-done | bytes 262168
  89.6 0.8 copy-done.3
  91.1 1.0 %coupling.1.rest_ref = f32[128,128]{1,0:T(8,128)S(1)} custom-call(s32[4]{0:T(128)S(1)} %bitcast.16, s32[8]{0:T(128)S(1)} %iota_xor_fusion.refs_2_.devices, bf16[8,8,16,128]{3,2,1,0:T(8,128)(2,1)S(1)} %copy-done.1, bf16[8,8,16,128]{3,2,1,0:T(8,128)(2,1)S(1)} %collective-permute-done.13.next_ref, bf16[4,128,128]{2,1,0:T(8,128)(2,1)S(1)} %bitcast.9, ...), custom_call_target="tpu_custom_call" | custom-call | tf_op jit(solution)/shard_map/coupling/pallas_call | solution.py:241
  92.1 1.3 %update.1 = f32[128,128]{1,0:T(8,128)} custom-call(s32[2]{0:T(128)S(1)} %dynamic-slice_reduce_fusion.atoms, bf16[8,128,128]{2,1,0:T(8,128)(2,1)S(1)} %all-to-all-done.1.terms_ref, f32[128,128]{1,0:T(8,128)S(1)} %coupling.1.rest_ref, f32[1,128]{1,0:T(1,128)S(1)} %copy-done.8, f32[128,1]{1,0:T(8,128)S(1)} %copy.15.down.down_ref, f32[1]{0:T(128)S(6)} %copy.34.shift), custom_call_target="tpu_custom_call" | custom-call | tf_op jit(solution)/shard_map/update/pallas_call | solution.py:306
  (70 shorter events, 14.4 us)
Async XLA Ops:
  0.0 5.0 %collective-permute-start.1 = (bf16[1,256,128]{2,1,0:T(8,128)(2,1)}, bf16[1,256,128]{2,1,0:T(8,128)(2,1)S(1)}, u32[]{:S(2)}, u32[]{:S(2)}) collective-permute-start(bf16[1,256,128]{2,1,0:T(8,128)(2,1)} %param.10), channel_id=1, source_target_pairs={{0,4},{1,5},{2,6},{3,7},{4,0},{5,1},{6,2},{7,3},{8,12},{9,13},{10,... | collective-permute-start | bytes 196616 | tf_op jit(solution)/shard_map/ppermute | solution.py:29
  3.1 6.8 %collective-permute-start = (bf16[1,128,128]{2,1,0:T(8,128)(2,1)}, bf16[1,128,128]{2,1,0:T(8,128)(2,1)S(1)}, u32[]{:S(2)}, u32[]{:S(2)}) collective-permute-start(bf16[1,128,128]{2,1,0:T(8,128)(2,1)} %param.9), channel_id=1, source_target_pairs={{0,4},{1,5},{2,6},{3,7},{4,0},{5,1},{6,2},{7,3},{8,12},{9,13},{10,... | collective-permute-start | bytes 98312 | tf_op jit(solution)/shard_map/ppermute | solution.py:29
  5.0 5.7 %collective-permute-start.2 = (bf16[2,256,128]{2,1,0:T(8,128)(2,1)S(1)}, bf16[2,256,128]{2,1,0:T(8,128)(2,1)S(1)}, u32[]{:S(2)}, u32[]{:S(2)}) collective-permute-start(bf16[2,256,128]{2,1,0:T(8,128)(2,1)S(1)} %constant_dynamic-update-slice_fusion.refs_1_), channel_id=1, source_target_pairs={{0,1},{1,0},{2,3},{3,2},{4,5},{5,4},{6,7},{7,6},{8,9},{9,8},{10,11... | collective-permute-start | bytes 393224 | tf_op jit(solution)/shard_map/ppermute | solution.py:29
  6.4 8.0 %collective-permute-start.6 = (bf16[2,256,128]{2,1,0:T(8,128)(2,1)S(1)}, bf16[2,256,128]{2,1,0:T(8,128)(2,1)S(1)}, u32[]{:S(2)}, u32[]{:S(2)}) collective-permute-start(bf16[2,256,128]{2,1,0:T(8,128)(2,1)S(1)} %constant_dynamic-update-slice_fusion.refs_1_), channel_id=1, source_target_pairs={{0,2},{1,3},{2,0},{3,1},{4,6},{5,7},{6,4},{7,5},{8,10},{9,11},{10,... | collective-permute-start | bytes 393224 | tf_op jit(solution)/shard_map/ppermute | solution.py:29
  9.9 6.0 %collective-permute-start.7 = (bf16[2,256,128]{2,1,0:T(8,128)(2,1)S(1)}, bf16[2,256,128]{2,1,0:T(8,128)(2,1)S(1)}, u32[]{:S(2)}, u32[]{:S(2)}) collective-permute-start(bf16[2,256,128]{2,1,0:T(8,128)(2,1)S(1)} %constant_dynamic-update-slice_fusion.refs_1_), channel_id=1, source_target_pairs={{0,3},{1,2},{2,1},{3,0},{4,7},{5,6},{6,5},{7,4},{8,11},{9,10},{10,... | collective-permute-start | bytes 393224 | tf_op jit(solution)/shard_map/ppermute | solution.py:29
  9.9 12.1 %copy-start.9 = (s32[3]{0:T(128)}, s32[3]{0:T(128)S(1)}, u32[]{:S(2)}) copy-start(s32[3]{0:T(128)S(1)} %get-tuple-element.20.refs_0_) | copy-start | bytes 40
  10.7 11.3 %collective-permute-start.3 = (bf16[2,128,128]{2,1,0:T(8,128)(2,1)S(1)}, bf16[2,128,128]{2,1,0:T(8,128)(2,1)S(1)}, u32[]{:S(2)}, u32[]{:S(2)}) collective-permute-start(bf16[2,128,128]{2,1,0:T(8,128)(2,1)S(1)} %pad_maximum_fusion.refs_3_), channel_id=1, source_target_pairs={{0,1},{1,0},{2,3},{3,2},{4,5},{5,4},{6,7},{7,6},{8,9},{9,8},{10,11... | collective-permute-start | bytes 196616 | tf_op jit(solution)/shard_map/ppermute | solution.py:29
  11.9 10.1 %collective-permute-start.4 = (bf16[2,128,128]{2,1,0:T(8,128)(2,1)S(1)}, bf16[2,128,128]{2,1,0:T(8,128)(2,1)S(1)}, u32[]{:S(2)}, u32[]{:S(2)}) collective-permute-start(bf16[2,128,128]{2,1,0:T(8,128)(2,1)S(1)} %pad_maximum_fusion.refs_3_), channel_id=1, source_target_pairs={{0,2},{1,3},{2,0},{3,1},{4,6},{5,7},{6,4},{7,5},{8,10},{9,11},{10,... | collective-permute-start | bytes 196616 | tf_op jit(solution)/shard_map/ppermute | solution.py:29
  14.3 7.7 %collective-permute-start.5 = (bf16[2,128,128]{2,1,0:T(8,128)(2,1)S(1)}, bf16[2,128,128]{2,1,0:T(8,128)(2,1)S(1)}, u32[]{:S(2)}, u32[]{:S(2)}) collective-permute-start(bf16[2,128,128]{2,1,0:T(8,128)(2,1)S(1)} %pad_maximum_fusion.refs_3_), channel_id=1, source_target_pairs={{0,3},{1,2},{2,1},{3,0},{4,7},{5,6},{6,5},{7,4},{8,11},{9,10},{10,... | collective-permute-start | bytes 196616 | tf_op jit(solution)/shard_map/ppermute | solution.py:29
  15.9 16.2 %copy-start.8 = (f32[1,128]{1,0:T(1,128)S(1)}, f32[1,128]{1,0:T(1,128)}, u32[]{:S(2)}) copy-start(f32[1,128]{1,0:T(1,128)} %across_ref.1) | copy-start | bytes 1540
  15.9 22.6 %copy-start.2 = (f32[1,128,128]{2,1,0:T(8,128)S(1)}, f32[1,128,128]{2,1,0:T(8,128)}, u32[]{:S(2)}) copy-start(f32[1,128,128]{2,1,0:T(8,128)} %param.13) | copy-start | bytes 196612
  22.0 16.5 %copy-start = (bf16[1,4,128,128]{3,2,1,0:T(8,128)(2,1)S(1)}, bf16[1,4,128,128]{3,2,1,0:T(8,128)(2,1)}, u32[]{:S(2)}) copy-start(bf16[1,4,128,128]{3,2,1,0:T(8,128)(2,1)} %param.12) | copy-start | bytes 393220
  22.0 10.0 %copy-start.4 = (bf16[2,128,128]{2,1,0:T(8,128)(2,1)}, bf16[2,128,128]{2,1,0:T(8,128)(2,1)S(1)}, u32[]{:S(2)}) copy-start(bf16[2,128,128]{2,1,0:T(8,128)(2,1)S(1)} %collective-permute-done.4.refs_5_) | copy-start | bytes 196612
  22.0 4.3 %copy-start.6 = (bf16[2,128,128]{2,1,0:T(8,128)(2,1)}, bf16[2,128,128]{2,1,0:T(8,128)(2,1)S(1)}, u32[]{:S(2)}) copy-start(bf16[2,128,128]{2,1,0:T(8,128)(2,1)S(1)} %collective-permute-done.5.refs_6_) | copy-start | bytes 196612
  27.0 11.5 %collective-permute-start.8 = (bf16[8,128,128]{2,1,0:T(8,128)(2,1)}, bf16[8,128,128]{2,1,0:T(8,128)(2,1)}, u32[]{:S(2)}, u32[]{:S(2)}) collective-permute-start(bf16[8,128,128]{2,1,0:T(8,128)(2,1)} %constant_dynamic-update-slice_fusion.2.own_ref), channel_id=1, source_target_pairs={{8,0},{16,8},{24,16},{9,1},{17,9},{25,17},{10,2},{18,10},{26,18},{... | collective-permute-start | bytes 786440 | tf_op jit(solution)/shard_map/ppermute | solution.py:48
  32.8 0.8 copy-start.5
  33.7 0.8 copy-start.7
  34.5 0.6 copy-start.10
  38.5 0.7 copy-start.12
  41.3 14.0 %all-to-all-start = ((bf16[8,5,16,128]{3,2,1,0:T(8,128)(2,1)}), bf16[8,5,16,128]{3,2,1,0:T(8,128)(2,1)S(1)}, u32[]{:S(2)}, u32[]{:S(2)}) async-start(bf16[8,5,16,128]{3,2,1,0:T(8,128)(2,1)} %scatter_rows.1), calls=%async_computation | async-start | bytes 327680 | tf_op jit(solution)/shard_map/all_to_all | solution.py:52
  56.1 3.7 %collective-permute-start.9 = (bf16[1,8,16,128]{3,2,1,0:T(8,128)(2,1)S(1)}, bf16[1,8,16,128]{3,2,1,0:T(8,128)(2,1)S(1)}, u32[]{:S(2)}, u32[]{:S(2)}) collective-permute-start(bf16[1,8,16,128]{3,2,1,0:T(8,128)(2,1)S(1)} %bitcast.10), channel_id=1, source_target_pairs={{0,4},{1,5},{2,6},{3,7},{4,0},{5,1},{6,2},{7,3},{8,12},{9,13},{10,... | collective-permute-start | bytes 98312 | tf_op jit(solution)/shard_map/ppermute | solution.py:29
  59.8 3.4 %copy-start.14 = (bf16[1,8,16,128]{3,2,1,0:T(8,128)(2,1)}, bf16[1,8,16,128]{3,2,1,0:T(8,128)(2,1)S(1)}, u32[]{:S(2)}) copy-start(bf16[1,8,16,128]{3,2,1,0:T(8,128)(2,1)S(1)} %collective-permute-done.9) | copy-start | bytes 98308
  59.8 3.3 %collective-permute-start.10 = (bf16[2,8,16,128]{3,2,1,0:T(8,128)(2,1)S(1)}, bf16[2,8,16,128]{3,2,1,0:T(8,128)(2,1)S(1)}, u32[]{:S(2)}, u32[]{:S(2)}) collective-permute-start(bf16[2,8,16,128]{3,2,1,0:T(8,128)(2,1)S(1)} %pad_maximum_fusion.1.refs_3_), channel_id=1, source_target_pairs={{0,1},{1,0},{2,3},{3,2},{4,5},{5,4},{6,7},{7,6},{8,9},{9,8},{10,11... | collective-permute-start | bytes 196616 | tf_op jit(solution)/shard_map/ppermute | solution.py:29
  59.9 3.3 %collective-permute-start.11 = (bf16[2,8,16,128]{3,2,1,0:T(8,128)(2,1)S(1)}, bf16[2,8,16,128]{3,2,1,0:T(8,128)(2,1)S(1)}, u32[]{:S(2)}, u32[]{:S(2)}) collective-permute-start(bf16[2,8,16,128]{3,2,1,0:T(8,128)(2,1)S(1)} %pad_maximum_fusion.1.refs_3_), channel_id=1, source_target_pairs={{0,2},{1,3},{2,0},{3,1},{4,6},{5,7},{6,4},{7,5},{8,10},{9,11},{10,... | collective-permute-start | bytes 196616 | tf_op jit(solution)/shard_map/ppermute | solution.py:29
  60.9 4.1 %collective-permute-start.12 = (bf16[2,8,16,128]{3,2,1,0:T(8,128)(2,1)S(1)}, bf16[2,8,16,128]{3,2,1,0:T(8,128)(2,1)S(1)}, u32[]{:S(2)}, u32[]{:S(2)}) collective-permute-start(bf16[2,8,16,128]{3,2,1,0:T(8,128)(2,1)S(1)} %pad_maximum_fusion.1.refs_3_), channel_id=1, source_target_pairs={{0,3},{1,2},{2,1},{3,0},{4,7},{5,6},{6,5},{7,4},{8,11},{9,10},{10,... | collective-permute-start | bytes 196616 | tf_op jit(solution)/shard_map/ppermute | solution.py:29
  65.0 0.6 copy-start.11
  68.9 23.2 %all-to-all-start.1 = ((bf16[8,128,128]{2,1,0:T(8,128)(2,1)}), bf16[8,128,128]{2,1,0:T(8,128)(2,1)S(1)}, u32[]{:S(2)}, u32[]{:S(2)}) async-start(bf16[8,128,128]{2,1,0:T(8,128)(2,1)} %ladder.3), calls=%async_computation.1 | async-start | bytes 524288 | tf_op jit(solution)/shard_map/all_to_all | solution.py:52
  77.4 11.3 %collective-permute-start.13 = (bf16[8,8,16,128]{3,2,1,0:T(8,128)(2,1)}, bf16[8,8,16,128]{3,2,1,0:T(8,128)(2,1)S(1)}, u32[]{:S(2)}, u32[]{:S(2)}) collective-permute-start(bf16[8,8,16,128]{3,2,1,0:T(8,128)(2,1)} %constant_dynamic-update-slice_fusion.10.own_ref), channel_id=1, source_target_pairs={{8,0},{16,8},{24,16},{9,1},{17,9},{25,17},{10,2},{18,10},{26,18},{... | collective-permute-start | bytes 786440 | tf_op jit(solution)/shard_map/ppermute | solution.py:48
  88.6 1.0 %copy-start.1 = (bf16[8,8,16,128]{3,2,1,0:T(8,128)(2,1)S(1)}, bf16[8,8,16,128]{3,2,1,0:T(8,128)(2,1)}, u32[]{:S(2)}) copy-start(bf16[8,8,16,128]{3,2,1,0:T(8,128)(2,1)} %constant_dynamic-update-slice_fusion.10.own_ref) | copy-start | bytes 786436
  89.6 0.8 copy-start.3
  90.4 0.7 copy-start.13
